TPU v7x, 32 devices: a whole 2x2x4 slice. The times are simulated.
32 devices in a mesh: space: 2 (over x), tm: 16 (over z, y, core).
Axes of the slice: x: 2, y: 2, z: 4, core: 2. Of those that a mesh axis runs over, the one named last changes fastest.
Arguments:
- record: float32 [3072, 8192], P('tm', 'space'), may hold values from -40 to 40
- mode_basis: float32 [21, 48, 48], replicated, may hold values from -0.2 to 1.2
- slow_picks: int32 [21, 32], replicated, may hold values from 0 to 47, all different within a row
- phases: int32 [21], replicated, may hold values from 0 to 3
Outputs:
- residual_record: float32 [3072, 8192], P('tm', 'space')
Inputs may be any that keep to these rules, and one draw needn't show every extreme that they name: `slow_picks`: the 32 entries of a row are different.
All inputs are finite; a program needn't handle non-finite values.
Results may differ from a plain program's by a relative error of at most 0.003.
Values may be sent and summed in bfloat16 or wider, within the bound.
No kernel may reach another device: no remote copies, remote signals or barrier semaphores. Data moves between devices by JAX's collectives and lax.ppermute only.
A program may use at most 64 MiB of HBM per device.

v0:
```python
import jax
import jax.numpy as jnp
from jax import lax
from jax.sharding import PartitionSpec as P

precise = lax.Precision.HIGHEST


def choose_columns(basis_w, picks_w, gram, points):
    size_m = basis_w.shape[1]
    modes_r = picks_w.shape[1]
    onehot = (picks_w[:, :, None] == jnp.arange(size_m, dtype=jnp.int32)[None, None, :]).astype(
        jnp.float32
    )
    chosen = jnp.einsum("wmn,wrn->wmr", basis_w, onehot, precision=precise)
    inner = jnp.einsum("wmn,wnr->wmr", gram, chosen, precision=precise)
    kernel = (
        jnp.einsum("wmr,wms->wrs", chosen, inner, precision=precise)
        + 1e-05 * jnp.eye(modes_r, dtype=jnp.float32)[None]
    )
    factor = jnp.linalg.cholesky(kernel)
    solved = lax.linalg.triangular_solve(
        factor, chosen, left_side=False, lower=True, transpose_a=True
    )
    return solved / jnp.sqrt(jnp.asarray(points, jnp.float32))


def project(modes, segments):
    partial_amp = jnp.einsum("wrp,wtp->wrt", modes, segments, precision=precise)
    return lax.psum(partial_amp, "space")


def remove_slow(segments, amplitude, modes):
    return segments - jnp.einsum("wrt,wrp->wtp", amplitude, modes, precision=precise)


def local_level(samples, basis_w, picks_w, segments, points):
    widened = samples.astype(jnp.float32)
    gram_part = jnp.einsum("wmp,wnp->wmn", samples, samples, preferred_element_type=jnp.float32)
    gram_total = lax.psum(gram_part, "space")
    weights = choose_columns(basis_w, picks_w, gram_total / points, points)
    modes = jnp.einsum("wmr,wmp->wrp", weights, widened, precision=precise)
    amplitude = project(modes, segments)
    return remove_slow(segments, amplitude, modes)


def body(record, mode_basis, slow_picks, phases):
    steps_dev, points_dev = record.shape
    size_m = mode_basis.shape[1]
    time_groups = lax.axis_size("tm")
    points = points_dev * lax.axis_size("space")
    position = lax.axis_index("tm")
    field = record
    offset_base = 0
    for level in range(3):
        window_count = 4**level
        stride = steps_dev * time_groups // (window_count * size_m)
        segment_count = max(1, window_count // time_groups)
        seglen = steps_dev // segment_count
        if window_count >= time_groups:
            first_win = position * segment_count
        else:
            first_win = position // (time_groups // window_count)
        owned_ids = first_win + jnp.arange(segment_count, dtype=jnp.int32)
        level_phases = phases[offset_base : offset_base + window_count]
        matches = (owned_ids[:, None] == jnp.arange(window_count, dtype=jnp.int32)[None, :]).astype(
            jnp.int32
        )
        offsets = jnp.sum(matches * level_phases[None, :], axis=1) % stride
        select = (jnp.arange(stride, dtype=jnp.int32)[None, :] == offsets[:, None]).astype(
            jnp.float32
        )
        shaped = field.reshape(segment_count, seglen // stride, stride, points_dev)
        sampled = jnp.sum(shaped * select[:, None, :, None], axis=2).astype(jnp.bfloat16)
        segments = field.reshape(segment_count, seglen, points_dev)
        level_basis = mode_basis[offset_base : offset_base + window_count]
        level_picks = slow_picks[offset_base : offset_base + window_count]
        if window_count >= time_groups:
            basis_w = lax.dynamic_slice_in_dim(level_basis, first_win, segment_count, 0)
            picks_w = lax.dynamic_slice_in_dim(level_picks, first_win, segment_count, 0)
            field = local_level(sampled, basis_w, picks_w, segments, points).reshape(
                steps_dev, points_dev
            )
        else:
            gathered = lax.all_gather(sampled[0], "tm", axis=0, tiled=True)
            own_rows = lax.dynamic_slice_in_dim(gathered, first_win * size_m, size_m, 0)[None]
            basis_w = lax.dynamic_slice_in_dim(level_basis, first_win, 1, 0)
            picks_w = lax.dynamic_slice_in_dim(level_picks, first_win, 1, 0)
            field = local_level(own_rows, basis_w, picks_w, segments, points).reshape(
                steps_dev, points_dev
            )
        offset_base = offset_base + window_count
    return field


def solution(mesh):
    in_specs = (P("tm", "space"), P(), P(), P())
    out_specs = P("tm", "space")
    return jax.shard_map(body, mesh=mesh, in_specs=in_specs, out_specs=out_specs, check_vma=False)
```

profile of v0, /device:TPU:0, one launch (start us, length us, event | category | flops | bytes accessed | tf_op | source)
XLA Modules:
  0.0 223.8 jit_solution(14836685744431826598)
XLA Ops:
  7.2 1.4 fusion.58
  10.6 2.4 %multiply_reduce_fusion.2 = bf16[3,4096]{1,0:T(4,128)(2,1)S(1)} fusion(f32[1,3,64,4096]{3,2,1,0:T(8,128)} %bitcast.161, f32[64]{0:T(128)S(1)} %compare_convert_fusion.2), kind=kLoop, calls=%fused_computation.5 | loop fusion | flops 1560576 | bytes 3170560 | tf_op jit(solution)/shard_map/reduce_sum | solution.py:74
  13.0 26.1 %all-gather = bf16[16,3,4096]{2,1,0:T(4,128)(2,1)} all-gather(bf16[1,3,4096]{2,1,0:T(4,128)(2,1)S(1)} %bitcast.166), channel_id=1, replica_groups=mesh['space'=2,'tm'=16] {'tm'}, dimensions={0}, use_global_device_ids=true | all-gather | bytes 417792 | tf_op jit(solution)/shard_map/all_gather | solution.py:85
  39.1 1.4 reshape.499
  41.3 9.5 %psum.42 = f32[1,48,48]{2,1,0:T(8,128)} all-reduce(f32[1,48,48]{2,1,0:T(8,128)} %convolution_bitcast_fusion.2), channel_id=1, replica_groups=mesh['space'=2,'tm'=16] {'space'}, use_global_device_ids=true, to_apply=%region_1.2 | all-reduce | flops 2304 | bytes 18432 | tf_op jit(solution)/shard_map/psum | solution.py:40
  54.1 1.4 copy.18
  56.8 4.2 %custom-call.10 = f32[1,32,32]{2,1,0:T(8,128)} custom-call(f32[1,32,32]{2,1,0:T(8,128)} %fusion.36), custom_call_target="Cholesky" | custom-call | tf_op jit(solution)/shard_map/jit(cholesky)/cholesky | solution.py:21
  62.4 1.9 fusion.30
  64.3 3.8 %custom-call.11 = f32[1,1,32,32]{2,3,1,0:T(8,128)} custom-call(f32[1,1,32,32]{3,2,1,0:T(8,128)} %fusion.30), custom_call_target="InvertDiagBlocksLowerTriangular" | custom-call | tf_op jit(solution)/shard_map/triangular_solve/custom-call.0 | solution.py:22
  70.2 2.9 %fusion.64 = f32[32,192]{1,0:T(8,128)S(1)} fusion(f32[32,4096]{1,0:T(8,128)S(1)} %fusion.63, f32[192,4096]{1,0:T(8,128)S(1)} %copy-done.1), kind=kOutput, calls=%fused_computation.104 | convolution fusion | flops 301989888 | bytes 3694592 | tf_op jit(solution)/shard_map/wrp,wtp->wrt/dot_general | solution.py:29
  73.1 7.4 %psum.43 = f32[32,192]{1,0:T(8,128)S(1)} all-reduce(f32[32,192]{1,0:T(8,128)S(1)} %fusion.64), channel_id=1, replica_groups=mesh['space'=2,'tm'=16] {'space'}, use_global_device_ids=true, to_apply=%region_4.7 | all-reduce | flops 6144 | bytes 49152 | tf_op jit(solution)/shard_map/psum | solution.py:30
  80.5 4.7 %convolution_subtract_fusion.2 = f32[192,4096]{1,0:T(8,128)S(1)} fusion(f32[192,4096]{1,0:T(8,128)} %param.7, f32[32,192]{1,0:T(8,128)S(1)} %psum.43, f32[32,4096]{1,0:T(8,128)} %copy-done.3), kind=kOutput, calls=%fused_computation.2 | convolution fusion | flops 302776320 | bytes 6840320 | tf_op jit(solution)/shard_map/wrt,wrp->wtp/dot_general | solution.py:34
  89.3 1.8 slice.42
  92.7 32.7 %all-gather.4.cloned.1.call-done = bf16[16,12,4096]{2,1,0:T(8,128)(2,1)} async-done(((bf16[1,12,4096]{2,1,0:T(8,128)(2,1)}), bf16[16,12,4096]{2,1,0:T(8,128)(2,1)}) %all-gather.4.cloned.1.call-update) | async-done | bytes 1572880 | tf_op jit(solution)/shard_map/all_gather | solution.py:85
  125.4 3.6 %reshape.501 = bf16[192,4096]{1,0:T(8,128)(2,1)} reshape(bf16[16,12,4096]{2,1,0:T(8,128)(2,1)} %all-gather.4.cloned.1.call-done) | data formatting | bytes 3145728
  129.0 1.4 convolution_bitcast_fusion.1
  130.4 8.4 %psum.44 = f32[1,48,48]{2,1,0:T(8,128)S(1)} all-reduce(f32[1,48,48]{2,1,0:T(8,128)S(1)} %convolution_bitcast_fusion.1), channel_id=1, replica_groups=mesh['space'=2,'tm'=16] {'space'}, use_global_device_ids=true, to_apply=%region_7.10 | all-reduce | flops 2304 | bytes 18432 | tf_op jit(solution)/shard_map/psum | solution.py:40
  139.2 2.9 %custom-call.12 = f32[1,32,32]{2,1,0:T(8,128)S(1)} custom-call(f32[1,32,32]{2,1,0:T(8,128)S(1)} %fusion.34), custom_call_target="Cholesky" | custom-call | tf_op jit(solution)/shard_map/jit(cholesky)/cholesky | solution.py:21
  143.6 2.4 %custom-call.13 = f32[1,1,32,32]{2,3,1,0:T(8,128)S(1)} custom-call(f32[1,1,32,32]{3,2,1,0:T(8,128)S(1)} %fusion.31), custom_call_target="InvertDiagBlocksLowerTriangular" | custom-call | tf_op jit(solution)/shard_map/triangular_solve/custom-call.0 | solution.py:22
  148.4 2.9 %fusion.65 = f32[32,192]{1,0:T(8,128)S(1)} fusion(f32[32,4096]{1,0:T(8,128)S(1)} %fusion.6, f32[192,4096]{1,0:T(8,128)S(1)} %convolution_subtract_fusion.2), kind=kOutput, calls=%fused_computation.105 | convolution fusion | flops 301989888 | bytes 3694592 | tf_op jit(solution)/shard_map/wrp,wtp->wrt/dot_general | solution.py:29
  151.4 7.4 %psum.45 = f32[32,192]{1,0:T(8,128)S(1)} all-reduce(f32[32,192]{1,0:T(8,128)S(1)} %fusion.65), channel_id=1, replica_groups=mesh['space'=2,'tm'=16] {'space'}, use_global_device_ids=true, to_apply=%region_8.11 | all-reduce | flops 6144 | bytes 49152 | tf_op jit(solution)/shard_map/psum | solution.py:30
  158.8 5.4 %convolution_subtract_fusion.1 = f32[192,4096]{1,0:T(8,128)} fusion(f32[192,4096]{1,0:T(8,128)S(1)} %convolution_subtract_fusion.2, f32[32,192]{1,0:T(8,128)S(1)} %psum.45, f32[32,4096]{1,0:T(8,128)} %copy-done.4), kind=kOutput, calls=%fused_computation.1 | convolution fusion | flops 302776320 | bytes 6840320 | tf_op jit(solution)/shard_map/wrt,wrp->wtp/dot_general | solution.py:34
  164.1 4.8 %reshape_reshape.7 = f32[1,48,4,4096]{3,2,1,0:T(4,128)} reshape(f32[192,4096]{1,0:T(8,128)} %convolution_subtract_fusion.1) | data formatting | bytes 6291456 | tf_op jit(solution)/shard_map/reshape;reshape | solution.py:73
  168.9 4.2 %multiply_reduce_fusion = bf16[48,4096]{1,0:T(8,128)(2,1)S(1)} fusion(f32[1,48,4,4096]{3,2,1,0:T(4,128)} %reshape_reshape.7, f32[4]{0:T(128)} %compare_convert_fusion), kind=kLoop, calls=%fused_computation.3 | loop fusion | flops 1376256 | bytes 3538960 | tf_op jit(solution)/shard_map/reduce_sum | solution.py:74
  174.0 9.5 %psum.46 = f32[1,48,48]{2,1,0:T(8,128)} all-reduce(f32[1,48,48]{2,1,0:T(8,128)} %convolution_bitcast_fusion), channel_id=1, replica_groups=mesh['space'=2,'tm'=16] {'space'}, use_global_device_ids=true, to_apply=%region_11.14 | all-reduce | flops 2304 | bytes 18432 | tf_op jit(solution)/shard_map/psum | solution.py:40
  185.1 1.4 copy.22
  187.8 4.2 %custom-call.14 = f32[1,32,32]{2,1,0:T(8,128)} custom-call(f32[1,32,32]{2,1,0:T(8,128)} %fusion.33), custom_call_target="Cholesky" | custom-call | tf_op jit(solution)/shard_map/jit(cholesky)/cholesky | solution.py:21
  193.4 1.9 fusion.32
  195.3 3.8 %custom-call.15 = f32[1,1,32,32]{2,3,1,0:T(8,128)} custom-call(f32[1,1,32,32]{3,2,1,0:T(8,128)} %fusion.32), custom_call_target="InvertDiagBlocksLowerTriangular" | custom-call | tf_op jit(solution)/shard_map/triangular_solve/custom-call.0 | solution.py:22
  201.2 2.9 %fusion.66 = f32[32,192]{1,0:T(8,128)S(1)} fusion(f32[32,4096]{1,0:T(8,128)S(1)} %fusion.67, f32[192,4096]{1,0:T(8,128)S(1)} %copy-done), kind=kOutput, calls=%fused_computation.106 | convolution fusion | flops 301989888 | bytes 3694592 | tf_op jit(solution)/shard_map/wrp,wtp->wrt/dot_general | solution.py:29
  204.1 7.4 %psum.47 = f32[32,192]{1,0:T(8,128)S(1)} all-reduce(f32[32,192]{1,0:T(8,128)S(1)} %fusion.66), channel_id=1, replica_groups=mesh['space'=2,'tm'=16] {'space'}, use_global_device_ids=true, to_apply=%region_12.15 | all-reduce | flops 6144 | bytes 49152 | tf_op jit(solution)/shard_map/psum | solution.py:30
  211.6 5.4 %convolution_subtract_fusion = f32[192,4096]{1,0:T(8,128)} fusion(f32[192,4096]{1,0:T(8,128)S(1)} %copy-done, f32[32,192]{1,0:T(8,128)S(1)} %psum.47, f32[32,4096]{1,0:T(8,128)} %copy-done.2), kind=kOutput, calls=%fused_computation | convolution fusion | flops 302776320 | bytes 6840320 | tf_op jit(solution)/shard_map/wrt,wrp->wtp/dot_general | solution.py:34
  (56 shorter events, 24.1 us)
Async XLA Ops:
  6.5 118.9 %all-gather.4.cloned.1.call-start = ((), (), s32[]{:S(2)}) async-start(), calls=%async_computation | async-start | bytes 2228224 | tf_op jit(solution)/shard_map/all_gather | solution.py:85
  10.6 59.6 %copy-start.1 = (f32[192,4096]{1,0:T(8,128)S(1)}, f32[192,4096]{1,0:T(8,128)}, u32[]{:S(2)}) copy-start(f32[192,4096]{1,0:T(8,128)} %param.7) | copy-start | bytes 9437188
  69.4 0.8 copy-start.3
  85.2 1.4 copy-start.5
  85.2 1.4 copy-start.6
  85.3 6.3 %slice-start = ((f32[21,48,48]{2,1,0:T(8,128)}), f32[4,48,48]{2,1,0:T(8,128)S(1)}, s32[]{:S(2)}) async-start(f32[21,48,48]{2,1,0:T(8,128)} %param.8), calls=%async_computation.1 | async-start | bytes 196608 | tf_op jit(solution)/shard_map/slice | solution.py:76
  147.6 0.8 copy-start.4
  168.9 32.2 %copy-start = (f32[192,4096]{1,0:T(8,128)S(1)}, f32[192,4096]{1,0:T(8,128)}, u32[]{:S(2)}) copy-start(f32[192,4096]{1,0:T(8,128)} %convolution_subtract_fusion.1) | copy-start | bytes 9437188
  200.4 0.8 copy-start.2
Sparse Core Ops, SparseCore 0:
  86.7 38.6 all-gather.3
where the time goes:
time: 226 us; the launch traced here: 224 us
  blocking collectives  75.6 us (33%)
  other arithmetic  42.5 us (19%)
  matrix products  37.1 us (16%)
  waiting for transfers between devices  32.7 us (14%)
  between operations  18.3 us (8%)
  local copies, waits for them, and re-layouts  17.4 us (8%)
    all_gather x1, waiting for transfers between devices, body(): gathered = lax.all_gather(sampled[0], 'tm', axis=0, tiled=True)  32.7 us
    psum x3, blocking collectives, local_level(): gram_total = lax.psum(gram_part, 'space')  27.3 us
    all_gather x1, blocking collectives, body(): gathered = lax.all_gather(sampled[0], 'tm', axis=0, tiled=True)  26.1 us
    psum x3, blocking collectives, project(): return lax.psum(partial_amp, 'space')  22.2 us
    dot_general x3, matrix products, remove_slow(): jnp.einsum('wrt,wrp->wtp', amplitude, modes, precision=precise)  15.4 us
    another operation x9, other arithmetic, choose_columns(): factor = jnp.linalg.cholesky(kernel)  14.9 us
    another operation x6, other arithmetic, choose_columns(): lax.linalg.triangular_solve(factor, chosen, left_side=False, lower=True,...  14.4 us
    dot_general x3, matrix products, project(): partial_amp = jnp.einsum('wrp,wtp->wrt', modes, segments, precision=precise)  8.81 us
  transfers between devices with their start and end apart: 1, of which 1 were waited for; matrix products, arithmetic and copies ran while one was open for 2% of the time, Pallas kernels for 0%

commit v1 on v0

v1 whole, which is shorter than its diff:
```python
import functools

import jax
import jax.numpy as jnp
from jax import lax
from jax.experimental import pallas as pl
from jax.experimental.pallas import tpu as pltpu
from jax.sharding import PartitionSpec as P

EPS = 1e-05
HI = lax.Precision.HIGHEST
F32 = jnp.float32
BF16 = jnp.bfloat16
LANES = 128
ROWS = 8
MIB = 1024 * 1024


def dot_nn(a, b, precision=None):
    return lax.dot_general(
        a, b, (((1,), (0,)), ((), ())), precision=precision, preferred_element_type=F32
    )


def dot_nt(a, b, precision=None):
    return lax.dot_general(
        a, b, (((1,), (1,)), ((), ())), precision=precision, preferred_element_type=F32
    )


def dot_tn(a, b, precision=None):
    return lax.dot_general(
        a, b, (((0,), (0,)), ((), ())), precision=precision, preferred_element_type=F32
    )


def split2(x):
    high = x.astype(BF16)
    return high, (x - high.astype(F32)).astype(BF16)


def iota(shape, axis):
    return lax.broadcasted_iota(jnp.int32, shape, axis)


def pick_phase(phases_ref, window, stride):
    phases = phases_ref[...]
    here = iota(phases.shape, 1) == window
    return lax.rem(jnp.sum(jnp.where(here, phases, 0), axis=1, keepdims=True), stride)


def slab_kernel(stride0, x_hbm, slab_ref, sems):
    size = 4
    copies = [
        pltpu.make_async_copy(
            x_hbm.at[pl.ds(stride0 * i, size), :], slab_ref.at[pl.ds(size * i, size), :], sems.at[i]
        )
        for i in range(sems.shape[0])
    ]
    for copy in copies:
        copy.start()
    rows, cols = slab_ref.shape
    used = size * sems.shape[0]
    slab_ref[used:rows] = jnp.zeros((rows - used, cols), F32)
    for copy in copies:
        copy.wait()


def first_kernel(stride0, phases_ref, slab_ref, out_ref, wide_ref):
    rows, cols = slab_ref.shape
    chunks = cols // LANES
    count = out_ref.shape[0] // chunks
    held = wide_ref.shape[0] // chunks
    off = pick_phase(phases_ref, 0, stride0)
    line, place = iota((held, rows), 0), iota((held, rows), 1)
    pick = ((place == 4 * line + off) & (line < count)).astype(BF16)
    wide = 512
    for p in range(cols // wide):
        got = dot_nn(pick, slab_ref[:, p * wide:(p + 1) * wide].astype(BF16))
        for c in range(wide // LANES):
            wide_ref[pl.ds(p * wide // LANES + c, held, stride=chunks), :] = got[
                :, c * LANES:(c + 1) * LANES
            ]
    out_ref[...] = wide_ref[0:count * chunks].astype(BF16)


def local_kernel(strides, phases_ref, x_ref, own0_ref, round_ref, sel_ref, own_ref, wide_ref):
    pos = lax.axis_index("tm")
    steps, cols = x_ref.shape
    chunks = cols // LANES
    size_m = sel_ref.shape[0]
    size0 = own0_ref.shape[0]
    n1 = steps // strides[1]
    held = wide_ref.shape[0] // chunks
    off1 = pick_phase(phases_ref, 1 + lax.div(pos, 4), strides[1])
    off2 = pick_phase(phases_ref, 5 + pos, strides[2])
    line, place = iota((size_m + held, steps), 0), iota((size_m + held, steps), 1)
    second = line >= size_m
    line = jnp.where(second, line - size_m, line)
    target = jnp.where(second, line * strides[1] + off1, line * strides[2] + off2)
    pick = ((place == target) & jnp.logical_not(second & (line >= n1))).astype(BF16)
    parts = 8
    wide = cols // parts
    for p in range(parts):
        at = slice(p * wide, (p + 1) * wide)
        rounded = x_ref[:, at].astype(BF16)
        round_ref[:, at] = rounded
        got = dot_nn(pick, rounded)
        sel_ref[:, at] = got[0:size_m].astype(BF16)
        for c in range(wide // LANES):
            wide_ref[pl.ds(p * wide // LANES + c, held, stride=chunks), :] = got[
                size_m:size_m + held, c * LANES:(c + 1) * LANES
            ]
    own_ref[0:size0] = own0_ref[...]
    own_ref[size0:size0 + n1 * chunks] = wide_ref[0:n1 * chunks].astype(BF16)


def modes_kernel(strides, phases_ref, basis_hbm, picks_ref, bt_ref, bd_ref, bx_ref, basis_ref, sems):
    pos = lax.axis_index("tm")
    modes_r, steps = bx_ref.shape
    size_m = basis_ref.shape[1]
    n0, n1 = steps // strides[0], steps // strides[1]
    windows = [0, 1 + lax.div(pos, 4), 5 + pos]
    copies = [
        pltpu.make_async_copy(basis_hbm.at[windows[level]], basis_ref.at[level], sems.at[level])
        for level in range(3)
    ]
    for copy in copies:
        copy.start()
    lane = iota((1, size_m), 1)

    def placed(width, flips, base):
        order = jnp.zeros((1, size_m), jnp.int32)
        for b, flip in enumerate(flips):
            inside = (lane >= b * width) & (lane < (b + 1) * width)
            order = jnp.where(inside, (base ^ flip) * width + lane - b * width, order)
        return order

    flips0 = [(b // 8) + (b // 4 % 2) * 2 + (0, 4, 12, 8)[b % 4] for b in range(16)]
    flips1 = [(b // 2) + (b % 2) * 2 for b in range(4)]
    orders = [placed(n0, flips0, pos), placed(n1, flips1, lax.rem(pos, 4)), lane]
    for copy in copies:
        copy.wait()
    for level in range(3):
        picks = picks_ref[pl.ds(windows[level], 1), :]
        onehot = (iota((size_m, modes_r), 0) == picks).astype(F32)
        chosen = dot_nn(basis_ref[level], onehot, HI)
        shuffle = (iota((size_m, size_m), 0) == orders[level]).astype(F32)
        bt_ref[level] = dot_tn(chosen, shuffle, HI)
    off2 = pick_phase(phases_ref, windows[2], strides[2])
    place = (iota((size_m, steps), 1) == iota((size_m, steps), 0) * strides[2] + off2)
    bx_ref[...] = dot_nn(bt_ref[2], place.astype(F32), HI)
    bd_ref[...] = jnp.zeros(bd_ref.shape, F32)
    for level in range(3):
        bd_ref[level * modes_r:(level + 1) * modes_r, level * size_m:(level + 1) * size_m] = bt_ref[level]


def unpack(pieces, wide_ref, s_ref, count):
    at = 0
    for piece, first, last in pieces:
        wide_ref[at:at + last - first] = piece[first:last].astype(F32)
        at += last - first
    chunks = s_ref.shape[1] // LANES
    for c in range(chunks):
        s_ref[0:count, c * LANES:(c + 1) * LANES] = wide_ref[
            pl.ds(c, count, stride=chunks), :
        ].astype(BF16)


def gram_kernel(points, size0, sel_ref, *refs):
    near, far, (gram_ref, s_ref, wide_ref, gather_ref) = refs[:4], refs[4:7], refs[7:]
    count, cols = sel_ref.shape
    first = s_ref.shape[0] - 2 * count
    unpack([(piece, size0, piece.shape[0]) for piece in near], wide_ref, gather_ref, count)
    s = gather_ref[0:count]
    gram_ref[...] = dot_nt(s, s) * (1.0 / points)
    s_ref[first:first + count] = s
    s_ref[first + count:first + 2 * count] = sel_ref[...]
    pieces, left = [], first * (cols // LANES)
    for i in range(3):
        for piece, size in ((near[i], size0), (far[i], far[i].shape[0])):
            take = min(size, left)
            if take:
                pieces.append((piece, 0, take))
                left -= take
    unpack(pieces, wide_ref, s_ref, first)


def cross_kernel(points, size0, round_ref, early_ref, gram_ref, bd_ref, bx_ref, far2_ref, near3_ref, far3_ref,
                 w_ref, s_ref, wide_ref):
    r, steps = bx_ref.shape
    count = gram_ref.shape[0]
    first = early_ref.shape[0] - 2 * count
    chunks = early_ref.shape[1] // LANES
    done = (first - count // 2) * chunks - size0
    size = far2_ref.shape[0]
    unpack([(far2_ref, done, size), (near3_ref, 0, size0), (far3_ref, 0, size)], wide_ref, s_ref, count - first)
    s0 = jnp.concatenate([early_ref[0:first], s_ref[...]], axis=0)
    s = jnp.concatenate([s0, early_ref[first:]], axis=0)
    cross = dot_nt(s, jnp.concatenate([round_ref[...], s0], axis=0)) * (1.0 / points)
    b0, b1 = bd_ref[0:r, 0:count], bd_ref[r:2 * r, count:2 * count]
    wx = dot_nn(bd_ref[...], cross[:, 0:steps], HI)
    g0 = dot_nn(bd_ref[0:2 * r, 0:2 * count], cross[0:2 * count, steps:steps + count], HI)
    g1 = dot_nn(b1, gram_ref[...], HI)
    wy = dot_nt(b0, g0, HI)
    at1, at2 = steps, steps + r
    w_ref[:, 0:steps] = wx
    w_ref[0:r, at1:at1 + r] = wy[:, r:2 * r]
    w_ref[r:2 * r, at1:at1 + r] = dot_nt(g1, b1, HI)
    w_ref[2 * r:3 * r, at1:at1 + r] = wy[:, 0:r]
    w_ref[:, at2:at2 + r] = dot_nt(wx, bx_ref[...], HI)


def inverse4(p):
    a, b, d = p[0][0], p[1][0], p[1][1]
    e, f, g, h = p[2][0], p[3][0], p[2][1], p[3][1]
    u, v, w = p[2][2], p[3][2], p[3][3]
    i = 1.0 / (a * d - b * b)
    t00, t01 = (d * e - b * g) * i, (d * f - b * h) * i
    t10, t11 = (a * g - b * e) * i, (a * h - b * f) * i
    s00 = u - (e * t00 + g * t10)
    s01 = v - (e * t01 + g * t11)
    s11 = w - (f * t01 + h * t11)
    j = 1.0 / (s00 * s11 - s01 * s01)
    m22, m23, m33 = s11 * j, -(s01 * j), s00 * j
    y00, y01 = t00 * m22 + t01 * m23, t00 * m23 + t01 * m33
    y10, y11 = t10 * m22 + t11 * m23, t10 * m23 + t11 * m33
    m00 = d * i + (y00 * t00 + y01 * t01)
    m01 = (y00 * t10 + y01 * t11) - b * i
    m11 = a * i + (y10 * t10 + y11 * t11)
    return [
        [m00, m01, -y00, -y01],
        [m01, m11, -y10, -y11],
        [-y00, -y10, m22, m23],
        [-y01, -y11, m23, m33],
    ]


def along_lanes(tile, lane):
    return jnp.broadcast_to(tile[:, lane:lane + 1], tile.shape)


def along_rows(tile, row):
    return jnp.broadcast_to(tile[row:row + 1, :], tile.shape)


def sum4(terms):
    return (terms[0] + terms[1]) + (terms[2] + terms[3])


def eliminate(tiles, at, base, beside=None):
    groups, width = len(tiles), len(tiles[0])
    sub = iota((ROWS, LANES), 0)
    four = range(4)
    tiles = [list(row) for row in tiles]
    cols = [[along_lanes(tiles[g][at], base + j) for g in range(groups)] for j in four]
    pivot = [[along_rows(cols[j][0], i) for j in range(i + 1)] for i in four]
    for k in range(0, groups * ROWS, 4):
        home, first = k // ROWS, k % ROWS
        m = inverse4(pivot)
        if k + 4 < groups * ROWS:
            then, start = (k + 4) // ROWS, (k + 4) % ROWS
            left = [[along_rows(cols[j][then], start + i) for j in four] for i in four]
            diag = [along_lanes(tiles[then][at], base + k + 4 + j) for j in four]
            diag = [[along_rows(diag[j], start + i) for j in range(i + 1)] for i in four]
            mixed = [[sum4([m[a][j] * left[i][j] for j in four]) for i in four] for a in four]
            pivot = [
                [diag[i][j] - sum4([left[i][a] * mixed[a][j] for a in four]) for j in range(i + 1)]
                for i in four
            ]
        rows = [[along_rows(tiles[home][t], first + i) for t in range(width)] for i in four]
        news = [
            [sum4([m[i][j] * rows[j][t] for j in four]) for t in range(width)] for i in four
        ]
        for g in range(groups):
            for t in range(width):
                tile = tiles[g][t] - sum4([cols[j][g] * news[j][t] for j in four])
                if g == home:
                    for i in four:
                        tile = jnp.where(sub == first + i, news[i][t], tile)
                tiles[g][t] = tile
        if k + 4 < groups * ROWS:
            cols = [[along_lanes(tiles[g][at], base + k + 4 + j) for g in range(groups)] for j in four]
        if beside is not None:
            beside(k // 4)
    return tiles


def to_tiles(value):
    return [
        [
            value[g * ROWS:(g + 1) * ROWS, t * LANES:(t + 1) * LANES]
            for t in range(value.shape[1] // LANES)
        ]
        for g in range(value.shape[0] // ROWS)
    ]


def from_tiles(tiles):
    return jnp.concatenate([jnp.concatenate(row, axis=1) for row in tiles], axis=0)


def solve_kernel(w_ref, got_ref, bt_ref, x_ref, early_ref, last_ref, out_hbm, out_ref, z_ref, out_sems):
    r = bt_ref.shape[1]
    count = bt_ref.shape[2]
    steps, cols = x_ref.shape
    first = count - last_ref.shape[0]
    w = w_ref[...] + got_ref[...]
    lanes = w.shape[1]
    b0, b1, b2 = bt_ref[0], bt_ref[1], bt_ref[2]

    def eye_at(base, width):
        return jnp.where(iota((r, width), 0) + base == iota((r, width), 1), EPS, 0.0)

    at1, at2 = steps, steps + r
    a0 = w[0:r]
    k0 = jnp.concatenate([w[2 * r:3 * r, at1:at1 + r], jnp.zeros((r, LANES - r), F32)], axis=1)
    k0 = k0 + eye_at(0, LANES)
    solved = eliminate(to_tiles(jnp.concatenate([a0, k0], axis=1)), lanes // LANES, 0)
    v0 = from_tiles([row[0:lanes // LANES] for row in solved])
    t0 = a0 + EPS * v0
    a1 = w[r:2 * r] - dot_tn(v0[:, at1:at1 + r], t0, HI)
    part2 = w[2 * r:3 * r] - dot_tn(v0[:, at2:at2 + r], t0, HI)
    v1 = from_tiles(eliminate(to_tiles(a1 + eye_at(at1, lanes)), at1 // LANES, at1 % LANES))
    t1 = a1 + EPS * v1
    a2 = part2 - dot_tn(v1[:, at2:at2 + r], t1, HI)
    v0 = v0 - dot_nn(v0[:, at1:at1 + r], v1, HI)
    early = jnp.concatenate(
        [dot_tn(v0[:, 0:steps], b0, HI), dot_tn(v1[:, 0:steps], b1, HI)], axis=1
    )
    early = jnp.concatenate(split2(early), axis=0)
    turn = jnp.concatenate(
        [-dot_tn(v0[:, at2:at2 + r], b0, HI), -dot_tn(v1[:, at2:at2 + r], b1, HI), b2], axis=1
    )
    turn = jnp.concatenate(split2(turn), axis=0)
    parts = r // 4
    wide = cols // parts

    def beside(p):
        at = slice(p * wide, (p + 1) * wide)
        s = jnp.concatenate(
            [early_ref[0:first, at], last_ref[:, at], early_ref[first:, at]], axis=0
        )
        slow = dot_nn(early, s[0:2 * count])
        out_ref[:, at] = x_ref[:, at] - (slow[0:steps] + slow[steps:2 * steps])
        both = dot_nn(turn, s)
        high, low = split2(both[0:r] + both[r:2 * r])
        z_ref[0:r, at] = high
        z_ref[r:2 * r, at] = high
        z_ref[2 * r:3 * r, at] = low

    tile2, lane2 = at2 // LANES, at2 % LANES
    v2 = from_tiles(eliminate(to_tiles(a2 + eye_at(at2, lanes)), tile2, lane2, beside))
    high = v2[:, 0:steps].astype(BF16).astype(F32)
    late = jnp.concatenate([high, v2[:, 0:steps] - high, high], axis=0).T.astype(BF16)
    copies = []
    parts = out_sems.shape[0]
    wide = cols // parts
    for p in range(parts):
        at = slice(p * wide, (p + 1) * wide)
        out_ref[:, at] = out_ref[:, at] - dot_nn(late, z_ref[:, at])
        copy = pltpu.make_async_copy(out_ref.at[:, at], out_hbm.at[:, at], out_sems.at[p])
        copy.start()
        copies.append(copy)
    for copy in copies:
        copy.wait()


def body(record, mode_basis, slow_picks, phases):
    steps, cols = record.shape
    size_m = mode_basis.shape[1]
    modes_r = slow_picks.shape[1]
    groups = lax.axis_size("tm")
    spaces = lax.axis_size("space")
    assert groups == 16 and cols % 512 == 0
    points = cols * spaces
    chunks = cols // LANES
    strides = tuple(steps * groups // (4**level * size_m) for level in range(3))
    n0, n1 = steps // strides[0], steps // strides[1]
    vmem = pl.BlockSpec(memory_space=pltpu.VMEM)
    hbm = pl.BlockSpec(memory_space=pltpu.HBM)

    def cost(flops, size):
        return pl.CostEstimate(flops=flops, bytes_accessed=size, transcendentals=0)

    def limit(size):
        return pltpu.CompilerParams(vmem_limit_bytes=size * MIB)

    def swap(value, bit):
        return lax.ppermute(value, "tm", [(i, i ^ bit) for i in range(groups)])

    def shape(rows, columns, dtype=F32):
        return jax.ShapeDtypeStruct((rows, columns), dtype)

    size0, size1 = n0 * chunks, n1 * chunks
    slab = pl.pallas_call(
        functools.partial(slab_kernel, strides[0]),
        out_shape=shape(16, cols),
        in_specs=[hbm],
        out_specs=vmem,
        scratch_shapes=[pltpu.SemaphoreType.DMA((n0,))],
        compiler_params=limit(53),
        cost_estimate=cost(0, 200000),
        name="sample_slabs",
    )(record)
    own0 = pl.pallas_call(
        functools.partial(first_kernel, strides[0]),
        out_shape=shape(size0, LANES, BF16),
        in_specs=[vmem, vmem],
        out_specs=vmem,
        scratch_shapes=[pltpu.VMEM((16 * chunks, LANES), F32)],
        compiler_params=limit(8),
        cost_estimate=cost(0, 200000),
        name="first_samples",
    )(phases[None], slab)

    z8, z4 = [swap(own0, bit) for bit in (8, 4)]
    rounded, sel, own = pl.pallas_call(
        functools.partial(local_kernel, strides),
        out_shape=(
            shape(steps, cols, BF16), shape(size_m, cols, BF16), shape(size0 + size1, LANES, BF16)
        ),
        in_specs=[vmem] * 3,
        out_specs=(vmem,) * 3,
        scratch_shapes=[pltpu.VMEM((16 * chunks, LANES), F32)],
        compiler_params=limit(12),
        cost_estimate=cost(1000, 1000),
        name="local_samples",
    )(phases[None], record, own0)
    own, z8 = lax.optimization_barrier((own, z8))
    z12 = swap(z8, 4)
    others = [z4, z12, z8]
    side, near = swap(own, 2), swap(own, 1)
    others, rounded, sel = lax.optimization_barrier((others, rounded, sel))
    far = jnp.concatenate(others, axis=0)
    side_far = swap(far, 2)
    far, phases_then = lax.optimization_barrier((far, phases))
    modes = pl.pallas_call(
        functools.partial(modes_kernel, strides),
        out_shape=(
            jax.ShapeDtypeStruct((3, modes_r, size_m), F32),
            shape(3 * modes_r, 3 * size_m),
            shape(modes_r, steps),
        ),
        in_specs=[vmem, hbm, vmem],
        out_specs=(vmem,) * 3,
        scratch_shapes=[
            pltpu.VMEM((3, size_m, size_m), F32),
            pltpu.SemaphoreType.DMA((3,)),
        ],
        compiler_params=limit(4),
        cost_estimate=cost(1000, 1000),
        name="chosen_modes",
    )(phases_then[None], mode_basis, slow_picks)

    side, modes = lax.optimization_barrier((side, modes))
    bt, bd, bx = modes
    near_far, next_side = swap(far, 1), swap(side, 1)
    own_then, side_far, near_far = lax.optimization_barrier((own, side_far, near_far))
    next_far = swap(side_far, 1)
    near = [own_then, side, near, next_side]
    first = 2 * size_m // 3 // 16 * 16
    gram, early = pl.pallas_call(
        functools.partial(gram_kernel, points, size0),
        out_shape=(shape(size_m, size_m), shape(first + 2 * size_m, cols, BF16)),
        in_specs=[vmem] * 8,
        out_specs=(vmem, vmem),
        scratch_shapes=[
            pltpu.VMEM((size_m * chunks, LANES), F32), pltpu.VMEM((size_m, cols), BF16)
        ],
        compiler_params=limit(8),
        cost_estimate=cost(1000, 1000),
        name="level_1_gram",
    )(sel, *near, far, side_far, near_far)
    next_far, gram, early = lax.optimization_barrier((next_far, gram, early))
    w, last = pl.pallas_call(
        functools.partial(cross_kernel, points, size0),
        out_shape=(
            shape(3 * modes_r, steps + 2 * modes_r), shape(size_m - first, cols, BF16)
        ),
        in_specs=[vmem] * 8,
        out_specs=(vmem, vmem),
        scratch_shapes=[pltpu.VMEM(((size_m - first) * chunks, LANES), F32)],
        compiler_params=limit(8),
        cost_estimate=cost(1000000000, 3000000),
        name="cross_products",
    )(rounded, early, gram, bd, bx, near_far, next_side, next_far)

    distance = 1
    other = jnp.zeros_like(w)
    while distance < spaces:
        other = lax.ppermute(w, "space", [(i, i ^ distance) for i in range(spaces)])
        distance *= 2
        if distance < spaces:
            w = w + other

    return pl.pallas_call(
        solve_kernel,
        out_shape=shape(steps, cols),
        in_specs=[vmem] * 6,
        out_specs=hbm,
        scratch_shapes=[
            pltpu.VMEM((steps, cols), F32),
            pltpu.VMEM((3 * modes_r, cols), BF16),
            pltpu.SemaphoreType.DMA((4,)),
        ],
        compiler_params=limit(16),
        cost_estimate=cost(1000000000, 9000000),
        name="remove_slow",
    )(w, other, bt, record, early, last)


def solution(mesh):
    in_specs = (P("tm", "space"), P(), P(), P())
    out_specs = P("tm", "space")
    return jax.shard_map(body, mesh=mesh, in_specs=in_specs, out_specs=out_specs, check_vma=False)
```

time: 226 us -> 30.8 us (0.14)
  blocking collectives: 75.6 us -> 0 us
  other arithmetic: 42.5 us -> 0 us
  matrix products: 37.1 us -> 0 us
  waiting for transfers between devices: 32.7 us -> 6.22 us
  between operations: 18.3 us -> 0.09 us
  local copies, waits for them, and re-layouts: 17.4 us -> 0.03 us
  starting transfers between devices: 0.01 us -> 12.6 us
  Pallas kernels: 0 us -> 11.7 us
    psum x6 -> x0, blocking collectives: 49.6 us -> none  [the longest x3 27.3 us: local_level(): gram_total = lax.psum(gram_part, 'space')]
    dot_general x21 -> x0, matrix products: 35 us -> none  [the longest x3 15.4 us: remove_slow(): jnp.einsum('wrt,wrp->wtp', amplitude, modes, precision=precise)]
    all_gather x1 -> x0, waiting for transfers between devices: 32.7 us -> none  [body(): gathered = lax.all_gather(sampled[0], 'tm', axis=0, tiled=True)]
    another operation x15 -> x0, other arithmetic: 29.3 us -> none  [the longest x9 14.9 us: choose_columns(): factor = jnp.linalg.cholesky(kernel)]
    all_gather x1 -> x0, blocking collectives: 26.1 us -> none  [body(): gathered = lax.all_gather(sampled[0], 'tm', axis=0, tiled=True)]
    ppermute x0 -> x10, starting transfers between devices: none -> 12.6 us  [the longest x9 11 us: swap(): return lax.ppermute(value, 'tm', [(i, i ^ bit) for i in range(groups)])]
    pallas_call x0 -> x7, Pallas kernels: none -> 11.7 us  [the longest x1 5.98 us: body(): pl.pallas_call(solve_kernel, out_shape=shape(steps, cols), in_specs=[vmem...]
    reduce_sum x5 -> x0, other arithmetic: 10 us -> none  [the longest x3 7.96 us: body(): jnp.sum(shaped * select[:, None, :, None], axis=2).astype(jnp.bfloat16)]
  transfers between devices with their start and end apart: 1 -> 10, of which waited for: 1 -> 4; matrix products, arithmetic and copies ran while one was open for 2% -> 0% of each run, Pallas kernels for 0% -> 8%
where the time goes in v1:
time: 30.8 us; the launch traced here: 30.6 us
  starting transfers between devices  12.6 us (41%)
  Pallas kernels  11.7 us (38%)
  waiting for transfers between devices  6.22 us (20%)
    ppermute x9, starting transfers between devices, swap(): return lax.ppermute(value, 'tm', [(i, i ^ bit) for i in range(groups)])  11 us
    pallas_call x1, Pallas kernels, body(): pl.pallas_call(solve_kernel, out_shape=shape(steps, cols), in_specs=[vmem...  5.98 us
    ppermute x1, waiting for transfers between devices, body(): other = lax.ppermute(w, 'space', [(i, i ^ distance) for i in range(spaces)])  3.55 us
    ppermute x9, waiting for transfers between devices, swap(): return lax.ppermute(value, 'tm', [(i, i ^ bit) for i in range(groups)])  2.67 us
    pallas_call x1, Pallas kernels, body(): pl.pallas_call(functools.partial(cross_kernel, points, size0), out_shape=...  1.85 us
    ppermute x1, starting transfers between devices, body(): other = lax.ppermute(w, 'space', [(i, i ^ distance) for i in range(spaces)])  1.59 us
    pallas_call x1, Pallas kernels, body(): pl.pallas_call(functools.partial(gram_kernel, points, size0), out_shape=(...  1.11 us
    pallas_call x1, Pallas kernels, body(): pl.pallas_call(functools.partial(slab_kernel, strides[0]), out_shape=shap...  1.09 us
  transfers between devices with their start and end apart: 10, of which 4 were waited for; matrix products, arithmetic and copies ran while one was open for 0% of the time, Pallas kernels for 8%

profile of v1, /device:TPU:0, one launch (start us, length us, event | category | flops | bytes accessed | tf_op | source)
XLA Modules:
  0.0 30.6 jit_solution(7594437534558173229)
XLA Ops:
  0.0 0.0 copy-start
  0.0 1.1 %sample_slabs.1.slab_ref = f32[16,4096]{1,0:T(8,128)S(1)} custom-call(f32[192,4096]{1,0:T(8,128)} %x_ref.3), custom_call_target="tpu_custom_call" | custom-call | bytes 200000 | tf_op jit(solution)/shard_map/sample_slabs/pallas_call | solution.py:396
  1.1 0.0 copy-done.3
  1.1 0.3 first_samples.1.own0_ref
  1.4 4.1 %collective-permute-start.1 = (bf16[96,128]{1,0:T(8,128)(2,1)S(1)}, bf16[96,128]{1,0:T(8,128)(2,1)S(1)}, u32[]{:S(2)}, u32[]{:S(2)}) collective-permute-start(bf16[96,128]{1,0:T(8,128)(2,1)S(1)} %first_samples.1.own0_ref), channel_id=1, source_target_pairs={{0,8},{1,9},{2,10},{3,11},{4,12},{5,13},{6,14},{7,15},{8,0},{9,1},... | collective-permute-start | bytes 73736 | tf_op jit(solution)/shard_map/ppermute | solution.py:390
  5.5 1.6 %collective-permute-start = (bf16[96,128]{1,0:T(8,128)(2,1)S(1)}, bf16[96,128]{1,0:T(8,128)(2,1)S(1)}, u32[]{:S(2)}, u32[]{:S(2)}) collective-permute-start(bf16[96,128]{1,0:T(8,128)(2,1)S(1)} %first_samples.1.own0_ref), channel_id=1, source_target_pairs={{0,4},{1,5},{2,6},{3,7},{4,0},{5,1},{6,2},{7,3},{8,12},{9,13},{10,... | collective-permute-start | bytes 73736 | tf_op jit(solution)/shard_map/ppermute | solution.py:390
  7.1 0.0 copy-done
  7.1 0.6 %local_samples.1 = (bf16[192,4096]{1,0:T(8,128)(2,1)S(1)}, bf16[48,4096]{1,0:T(8,128)(2,1)S(1)}, bf16[480,128]{1,0:T(8,128)(2,1)S(1)}) custom-call(s32[1,21]{1,0:T(1,128)S(1)} %bitcast.3, f32[192,4096]{1,0:T(8,128)S(1)} %copy-done, bf16[96,128]{1,0:T(8,128)(2,1)S(1)} %first_samples.1.own0_ref), custom_call_target="tpu_custom_call" | custom-call | flops 1000 | bytes 1000 | tf_op jit(solution)/shard_map/local_samples/pallas_call | solution.py:418
  7.7 0.0 collective-permute-done.1
  7.7 1.5 %collective-permute-start.2 = (bf16[96,128]{1,0:T(8,128)(2,1)S(1)}, bf16[96,128]{1,0:T(8,128)(2,1)S(1)}, u32[]{:S(2)}, u32[]{:S(2)}) collective-permute-start(bf16[96,128]{1,0:T(8,128)(2,1)S(1)} %collective-permute-done.1), channel_id=1, source_target_pairs={{0,4},{1,5},{2,6},{3,7},{4,0},{5,1},{6,2},{7,3},{8,12},{9,13},{10,... | collective-permute-start | bytes 73736 | tf_op jit(solution)/shard_map/ppermute | solution.py:390
  9.2 1.5 %collective-permute-start.6 = (bf16[480,128]{1,0:T(8,128)(2,1)S(1)}, bf16[480,128]{1,0:T(8,128)(2,1)S(1)}, u32[]{:S(2)}, u32[]{:S(2)}) collective-permute-start(bf16[480,128]{1,0:T(8,128)(2,1)S(1)} %get-tuple-element.46.refs_0_), channel_id=1, source_target_pairs={{0,2},{1,3},{2,0},{3,1},{4,6},{5,7},{6,4},{7,5},{8,10},{9,11},{10,... | collective-permute-start | bytes 368648 | tf_op jit(solution)/shard_map/ppermute | solution.py:390
  10.7 0.0 collective-permute-done
  10.7 0.9 %collective-permute-done.2 = bf16[96,128]{1,0:T(8,128)(2,1)S(1)} collective-permute-done((bf16[96,128]{1,0:T(8,128)(2,1)S(1)}, bf16[96,128]{1,0:T(8,128)(2,1)S(1)}, u32[]{:S(2)}, u32[]{:S(2)}) %collective-permute-start.2) | collective-permute-done | bytes 24608 | tf_op jit(solution)/shard_map/ppermute | solution.py:390
  11.6 0.1 collective-permute-start.4
  11.7 1.6 %collective-permute-start.3 = (bf16[288,128]{1,0:T(8,128)(2,1)S(1)}, bf16[288,128]{1,0:T(8,128)(2,1)S(1)}, u32[]{:S(2)}, u32[]{:S(2)}) collective-permute-start(bf16[288,128]{1,0:T(8,128)(2,1)S(1)} %constant_dynamic-update-slice_fusion.refs_4_), channel_id=1, source_target_pairs={{0,2},{1,3},{2,0},{3,1},{4,6},{5,7},{6,4},{7,5},{8,10},{9,11},{10,... | collective-permute-start | bytes 221192 | tf_op jit(solution)/shard_map/ppermute | solution.py:390
  13.3 0.2 collective-permute-start.7
  13.5 0.0 copy-done.2
  13.5 0.0 copy-done.1
  13.5 0.8 %chosen_modes.1 = (f32[3,32,48]{2,1,0:T(8,128)S(1)}, f32[96,144]{1,0:T(8,128)S(1)}, f32[32,192]{1,0:T(8,128)S(1)}) custom-call(s32[1,21]{1,0:T(1,128)S(1)} %bitcast.4, f32[21,48,48]{2,1,0:T(8,128)S(1)} %copy-done.1, s32[21,32]{1,0:T(8,128)S(1)} %copy-done.2), custom_call_target="tpu_custom_call" | custom-call | flops 1000 | bytes 1000 | tf_op jit(solution)/shard_map/chosen_modes/pallas_call | solution.py:438
  14.3 0.0 collective-permute-done.6.refs_1_
  14.3 0.4 %collective-permute-start.8 = (bf16[480,128]{1,0:T(8,128)(2,1)S(1)}, bf16[480,128]{1,0:T(8,128)(2,1)S(1)}, u32[]{:S(2)}, u32[]{:S(2)}) collective-permute-start(bf16[480,128]{1,0:T(8,128)(2,1)S(1)} %collective-permute-done.6.refs_1_), channel_id=1, source_target_pairs={{0,1},{1,0},{2,3},{3,2},{4,5},{5,4},{6,7},{7,6},{8,9},{9,8},{10,11... | collective-permute-start | bytes 368648 | tf_op jit(solution)/shard_map/ppermute | solution.py:390
  14.7 0.0 collective-permute-done.4.refs_6_.far2_ref
  14.7 1.7 %collective-permute-done.3.refs_5_ = bf16[288,128]{1,0:T(8,128)(2,1)S(1)} collective-permute-done((bf16[288,128]{1,0:T(8,128)(2,1)S(1)}, bf16[288,128]{1,0:T(8,128)(2,1)S(1)}, u32[]{:S(2)}, u32[]{:S(2)}) %collective-permute-start.3) | collective-permute-done | bytes 73760 | tf_op jit(solution)/shard_map/ppermute | solution.py:390
  16.4 0.0 collective-permute-start.5
  16.4 0.0 collective-permute-done.7.refs_2_
  16.4 0.0 collective-permute-done.8.refs_3_.near3_ref
  16.4 1.1 %level_1_gram.1 = (f32[48,48]{1,0:T(8,128)S(1)}, bf16[128,4096]{1,0:T(8,128)(2,1)S(1)}) custom-call(bf16[48,4096]{1,0:T(8,128)(2,1)S(1)} %get-tuple-element.45.sel_ref, bf16[480,128]{1,0:T(8,128)(2,1)S(1)} %get-tuple-element.46.refs_0_, bf16[480,128]{1,0:T(8,128)(2,1)S(1)} %collective-permute-done.6.refs_1_, ...), custom_call_target="tpu_custom_call" | custom-call | flops 1000 | bytes 1000 | tf_op jit(solution)/shard_map/level_1_gram/pallas_call | solution.py:463
  17.5 0.1 collective-permute-done.5.far3_ref
  17.6 1.9 %cross_products.1 = (f32[96,256]{1,0:T(8,128)S(1)}, bf16[16,4096]{1,0:T(8,128)(2,1)S(1)}) custom-call(bf16[192,4096]{1,0:T(8,128)(2,1)S(1)} %get-tuple-element.38.round_ref, bf16[128,4096]{1,0:T(8,128)(2,1)S(1)} %get-tuple-element.55.early_ref, f32[48,48]{1,0:T(8,128)S(1)} %get-tuple-element.56.gram_ref, f32[96,144]{1,0:T(8,128)S(1)} %get-tuple-element.57.bd_ref, ...), custom_call_target="tpu_custom_call" | custom-call | flops 1000000000 | bytes 3000000 | tf_op jit(solution)/shard_map/cross_products/pallas_call | solution.py:476
  19.5 1.6 %collective-permute-start.9 = (f32[96,256]{1,0:T(8,128)S(1)}, f32[96,256]{1,0:T(8,128)S(1)}, u32[]{:S(2)}, u32[]{:S(2)}) collective-permute-start(f32[96,256]{1,0:T(8,128)S(1)} %get-tuple-element.60.w_ref), channel_id=1, source_target_pairs={{0,16},{16,0},{1,17},{17,1},{2,18},{18,2},{3,19},{19,3},{4,20},{20... | collective-permute-start | bytes 294920 | tf_op jit(solution)/shard_map/ppermute | solution.py:492
  21.1 3.5 %collective-permute-done.9.got_ref = f32[96,256]{1,0:T(8,128)S(1)} collective-permute-done((f32[96,256]{1,0:T(8,128)S(1)}, f32[96,256]{1,0:T(8,128)S(1)}, u32[]{:S(2)}, u32[]{:S(2)}) %collective-permute-start.9) | collective-permute-done | bytes 98336 | tf_op jit(solution)/shard_map/ppermute | solution.py:492
  24.6 6.0 %remove_slow.1 = f32[192,4096]{1,0:T(8,128)} custom-call(f32[96,256]{1,0:T(8,128)S(1)} %get-tuple-element.60.w_ref, f32[96,256]{1,0:T(8,128)S(1)} %collective-permute-done.9.got_ref, f32[3,32,48]{2,1,0:T(8,128)S(1)} %get-tuple-element.61.bt_ref, f32[192,4096]{1,0:T(8,128)S(1)} %copy-done, bf16[128,4096]{1,0:T(8,128)(2,1)S(1)} %get-tuple-element.55.early_ref, ...), custom_call_target="tpu_custom_call" | custom-call | flops 1000000000 | bytes 9000000 | tf_op jit(solution)/shard_map/remove_slow/pallas_call | solution.py:497
  (6 shorter events, 0.0 us)
Async XLA Ops:
  0.0 7.1 %copy-start = (f32[192,4096]{1,0:T(8,128)S(1)}, f32[192,4096]{1,0:T(8,128)}, u32[]{:S(2)}) copy-start(f32[192,4096]{1,0:T(8,128)} %x_ref.3) | copy-start | bytes 9437188
  0.0 1.1 %copy-start.3 = (s32[21]{0:T(128)S(1)}, s32[21]{0:T(128)}, u32[]{:S(2)}) copy-start(s32[21]{0:T(128)} %param.7) | copy-start | bytes 256
  0.0 13.5 %copy-start.2 = (s32[21,32]{1,0:T(8,128)S(1)}, s32[21,32]{1,0:T(8,128)}, u32[]{:S(2)}) copy-start(s32[21,32]{1,0:T(8,128)} %picks_ref.1) | copy-start | bytes 8068
  0.0 13.5 %copy-start.1 = (f32[21,48,48]{2,1,0:T(8,128)S(1)}, f32[21,48,48]{2,1,0:T(8,128)}, u32[]{:S(2)}) copy-start(f32[21,48,48]{2,1,0:T(8,128)} %basis_hbm.1) | copy-start | bytes 580612
  1.4 6.3 %collective-permute-start.1 = (bf16[96,128]{1,0:T(8,128)(2,1)S(1)}, bf16[96,128]{1,0:T(8,128)(2,1)S(1)}, u32[]{:S(2)}, u32[]{:S(2)}) collective-permute-start(bf16[96,128]{1,0:T(8,128)(2,1)S(1)} %first_samples.1.own0_ref), channel_id=1, source_target_pairs={{0,8},{1,9},{2,10},{3,11},{4,12},{5,13},{6,14},{7,15},{8,0},{9,1},... | collective-permute-start | bytes 73736 | tf_op jit(solution)/shard_map/ppermute | solution.py:390
  5.5 5.2 %collective-permute-start = (bf16[96,128]{1,0:T(8,128)(2,1)S(1)}, bf16[96,128]{1,0:T(8,128)(2,1)S(1)}, u32[]{:S(2)}, u32[]{:S(2)}) collective-permute-start(bf16[96,128]{1,0:T(8,128)(2,1)S(1)} %first_samples.1.own0_ref), channel_id=1, source_target_pairs={{0,4},{1,5},{2,6},{3,7},{4,0},{5,1},{6,2},{7,3},{8,12},{9,13},{10,... | collective-permute-start | bytes 73736 | tf_op jit(solution)/shard_map/ppermute | solution.py:390
  7.7 3.9 %collective-permute-start.2 = (bf16[96,128]{1,0:T(8,128)(2,1)S(1)}, bf16[96,128]{1,0:T(8,128)(2,1)S(1)}, u32[]{:S(2)}, u32[]{:S(2)}) collective-permute-start(bf16[96,128]{1,0:T(8,128)(2,1)S(1)} %collective-permute-done.1), channel_id=1, source_target_pairs={{0,4},{1,5},{2,6},{3,7},{4,0},{5,1},{6,2},{7,3},{8,12},{9,13},{10,... | collective-permute-start | bytes 73736 | tf_op jit(solution)/shard_map/ppermute | solution.py:390
  9.2 5.1 %collective-permute-start.6 = (bf16[480,128]{1,0:T(8,128)(2,1)S(1)}, bf16[480,128]{1,0:T(8,128)(2,1)S(1)}, u32[]{:S(2)}, u32[]{:S(2)}) collective-permute-start(bf16[480,128]{1,0:T(8,128)(2,1)S(1)} %get-tuple-element.46.refs_0_), channel_id=1, source_target_pairs={{0,2},{1,3},{2,0},{3,1},{4,6},{5,7},{6,4},{7,5},{8,10},{9,11},{10,... | collective-permute-start | bytes 368648 | tf_op jit(solution)/shard_map/ppermute | solution.py:390
  11.6 3.1 %collective-permute-start.4 = (bf16[288,128]{1,0:T(8,128)(2,1)S(1)}, bf16[288,128]{1,0:T(8,128)(2,1)S(1)}, u32[]{:S(2)}, u32[]{:S(2)}) collective-permute-start(bf16[288,128]{1,0:T(8,128)(2,1)S(1)} %constant_dynamic-update-slice_fusion.refs_4_), channel_id=1, source_target_pairs={{0,1},{1,0},{2,3},{3,2},{4,5},{5,4},{6,7},{7,6},{8,9},{9,8},{10,11... | collective-permute-start | bytes 221192 | tf_op jit(solution)/shard_map/ppermute | solution.py:390
  11.7 4.7 %collective-permute-start.3 = (bf16[288,128]{1,0:T(8,128)(2,1)S(1)}, bf16[288,128]{1,0:T(8,128)(2,1)S(1)}, u32[]{:S(2)}, u32[]{:S(2)}) collective-permute-start(bf16[288,128]{1,0:T(8,128)(2,1)S(1)} %constant_dynamic-update-slice_fusion.refs_4_), channel_id=1, source_target_pairs={{0,2},{1,3},{2,0},{3,1},{4,6},{5,7},{6,4},{7,5},{8,10},{9,11},{10,... | collective-permute-start | bytes 221192 | tf_op jit(solution)/shard_map/ppermute | solution.py:390
  13.3 3.1 %collective-permute-start.7 = (bf16[480,128]{1,0:T(8,128)(2,1)S(1)}, bf16[480,128]{1,0:T(8,128)(2,1)S(1)}, u32[]{:S(2)}, u32[]{:S(2)}) collective-permute-start(bf16[480,128]{1,0:T(8,128)(2,1)S(1)} %get-tuple-element.46.refs_0_), channel_id=1, source_target_pairs={{0,1},{1,0},{2,3},{3,2},{4,5},{5,4},{6,7},{7,6},{8,9},{9,8},{10,11... | collective-permute-start | bytes 368648 | tf_op jit(solution)/shard_map/ppermute | solution.py:390
  14.3 2.1 %collective-permute-start.8 = (bf16[480,128]{1,0:T(8,128)(2,1)S(1)}, bf16[480,128]{1,0:T(8,128)(2,1)S(1)}, u32[]{:S(2)}, u32[]{:S(2)}) collective-permute-start(bf16[480,128]{1,0:T(8,128)(2,1)S(1)} %collective-permute-done.6.refs_1_), channel_id=1, source_target_pairs={{0,1},{1,0},{2,3},{3,2},{4,5},{5,4},{6,7},{7,6},{8,9},{9,8},{10,11... | collective-permute-start | bytes 368648 | tf_op jit(solution)/shard_map/ppermute | solution.py:390
  16.4 1.3 %collective-permute-start.5 = (bf16[288,128]{1,0:T(8,128)(2,1)S(1)}, bf16[288,128]{1,0:T(8,128)(2,1)S(1)}, u32[]{:S(2)}, u32[]{:S(2)}) collective-permute-start(bf16[288,128]{1,0:T(8,128)(2,1)S(1)} %collective-permute-done.3.refs_5_), channel_id=1, source_target_pairs={{0,1},{1,0},{2,3},{3,2},{4,5},{5,4},{6,7},{7,6},{8,9},{9,8},{10,11... | collective-permute-start | bytes 221192 | tf_op jit(solution)/shard_map/ppermute | solution.py:390
  19.5 5.1 %collective-permute-start.9 = (f32[96,256]{1,0:T(8,128)S(1)}, f32[96,256]{1,0:T(8,128)S(1)}, u32[]{:S(2)}, u32[]{:S(2)}) collective-permute-start(f32[96,256]{1,0:T(8,128)S(1)} %get-tuple-element.60.w_ref), channel_id=1, source_target_pairs={{0,16},{16,0},{1,17},{17,1},{2,18},{18,2},{3,19},{19,3},{4,20},{20... | collective-permute-start | bytes 294920 | tf_op jit(solution)/shard_map/ppermute | solution.py:492

commit v2 on v1

--- a/solution.py
+++ b/solution.py
@@ -300,7 +300,7 @@
     return jnp.concatenate([jnp.concatenate(row, axis=1) for row in tiles], axis=0)
 
 
-def solve_kernel(w_ref, got_ref, bt_ref, x_ref, early_ref, last_ref, out_hbm, out_ref, z_ref, out_sems):
+def solve_kernel(w_ref, got_ref, bt_ref, x_ref, early_ref, last_ref, out_hbm, out_ref, z1_ref, z2_ref, out_sems):
     r = bt_ref.shape[1]
     count = bt_ref.shape[2]
     steps, cols = x_ref.shape
@@ -313,52 +313,71 @@
         return jnp.where(iota((r, width), 0) + base == iota((r, width), 1), EPS, 0.0)
 
     at1, at2 = steps, steps + r
+    assert at1 // LANES == (at2 + r - 1) // LANES
     a0 = w[0:r]
-    k0 = jnp.concatenate([w[2 * r:3 * r, at1:at1 + r], jnp.zeros((r, LANES - r), F32)], axis=1)
-    k0 = k0 + eye_at(0, LANES)
-    solved = eliminate(to_tiles(jnp.concatenate([a0, k0], axis=1)), lanes // LANES, 0)
+    tile1, lane1 = at1 // LANES, at1 % LANES
+    tile2, lane2 = at2 // LANES, at2 % LANES
+    k0 = w[2 * r:3 * r] + eye_at(at1, lanes)
+    solved = eliminate(
+        to_tiles(jnp.concatenate([a0, k0[:, tile1 * LANES:(tile1 + 1) * LANES]], axis=1)),
+        lanes // LANES, lane1,
+    )
     v0 = from_tiles([row[0:lanes // LANES] for row in solved])
     t0 = a0 + EPS * v0
     a1 = w[r:2 * r] - dot_tn(v0[:, at1:at1 + r], t0, HI)
     part2 = w[2 * r:3 * r] - dot_tn(v0[:, at2:at2 + r], t0, HI)
-    v1 = from_tiles(eliminate(to_tiles(a1 + eye_at(at1, lanes)), at1 // LANES, at1 % LANES))
+    parts = r // 4
+    wide = cols // parts
+
+    def samples_at(at):
+        return jnp.concatenate(
+            [early_ref[0:first, at], last_ref[:, at], early_ref[first:, at]], axis=0
+        )
+
+    def keep(ref, at, both):
+        high, low = split2(both[0:r] + both[r:2 * r])
+        ref[0:r, at] = high
+        ref[r:2 * r, at] = high
+        ref[2 * r:3 * r, at] = low
+
+    def turned(value):
+        high = value.astype(BF16).astype(F32)
+        return jnp.concatenate([high, value - high, high], axis=0).T.astype(BF16)
+
+    v01 = v0[:, at1:at1 + r]
+    coef0 = jnp.concatenate(split2(dot_tn(v0[:, 0:steps], b0, HI)), axis=0)
+    turn1 = jnp.concatenate([-dot_tn(v01, b0, HI), b1], axis=1)
+    turn1 = jnp.concatenate(split2(turn1), axis=0)
+
+    def beside1(p):
+        at = slice(p * wide, (p + 1) * wide)
+        s = samples_at(at)
+        slow = dot_nn(coef0, s[0:count])
+        out_ref[:, at] = x_ref[:, at] - (slow[0:steps] + slow[steps:2 * steps])
+        keep(z1_ref, at, dot_nn(turn1, s[0:2 * count]))
+
+    v1 = from_tiles(eliminate(to_tiles(a1 + eye_at(at1, lanes)), tile1, lane1, beside1))
     t1 = a1 + EPS * v1
     a2 = part2 - dot_tn(v1[:, at2:at2 + r], t1, HI)
-    v0 = v0 - dot_nn(v0[:, at1:at1 + r], v1, HI)
-    early = jnp.concatenate(
-        [dot_tn(v0[:, 0:steps], b0, HI), dot_tn(v1[:, 0:steps], b1, HI)], axis=1
-    )
-    early = jnp.concatenate(split2(early), axis=0)
-    turn = jnp.concatenate(
-        [-dot_tn(v0[:, at2:at2 + r], b0, HI), -dot_tn(v1[:, at2:at2 + r], b1, HI), b2], axis=1
-    )
-    turn = jnp.concatenate(split2(turn), axis=0)
-    parts = r // 4
-    wide = cols // parts
-
-    def beside(p):
+    v12 = v1[:, at2:at2 + r]
+    v02 = v0[:, at2:at2 + r] - dot_nn(v01, v12, HI)
+    late1 = turned(v1[:, 0:steps])
+    turn2 = jnp.concatenate([-dot_tn(v02, b0, HI), -dot_tn(v12, b1, HI), b2], axis=1)
+    turn2 = jnp.concatenate(split2(turn2), axis=0)
+
+    def beside2(p):
         at = slice(p * wide, (p + 1) * wide)
-        s = jnp.concatenate(
-            [early_ref[0:first, at], last_ref[:, at], early_ref[first:, at]], axis=0
-        )
-        slow = dot_nn(early, s[0:2 * count])
-        out_ref[:, at] = x_ref[:, at] - (slow[0:steps] + slow[steps:2 * steps])
-        both = dot_nn(turn, s)
-        high, low = split2(both[0:r] + both[r:2 * r])
-        z_ref[0:r, at] = high
-        z_ref[r:2 * r, at] = high
-        z_ref[2 * r:3 * r, at] = low
-
-    tile2, lane2 = at2 // LANES, at2 % LANES
-    v2 = from_tiles(eliminate(to_tiles(a2 + eye_at(at2, lanes)), tile2, lane2, beside))
-    high = v2[:, 0:steps].astype(BF16).astype(F32)
-    late = jnp.concatenate([high, v2[:, 0:steps] - high, high], axis=0).T.astype(BF16)
+        out_ref[:, at] = out_ref[:, at] - dot_nn(late1, z1_ref[:, at])
+        keep(z2_ref, at, dot_nn(turn2, samples_at(at)))
+
+    v2 = from_tiles(eliminate(to_tiles(a2 + eye_at(at2, lanes)), tile2, lane2, beside2))
+    late2 = turned(v2[:, 0:steps])
     copies = []
     parts = out_sems.shape[0]
     wide = cols // parts
     for p in range(parts):
         at = slice(p * wide, (p + 1) * wide)
-        out_ref[:, at] = out_ref[:, at] - dot_nn(late, z_ref[:, at])
+        out_ref[:, at] = out_ref[:, at] - dot_nn(late2, z2_ref[:, at])
         copy = pltpu.make_async_copy(out_ref.at[:, at], out_hbm.at[:, at], out_sems.at[p])
         copy.start()
         copies.append(copy)
@@ -414,7 +433,8 @@
         name="first_samples",
     )(phases[None], slab)
 
-    z8, z4 = [swap(own0, bit) for bit in (8, 4)]
+    z8, z12, z4 = [swap(own0, bit) for bit in (8, 12, 4)]
+    others = [z4, z12, z8]
     rounded, sel, own = pl.pallas_call(
         functools.partial(local_kernel, strides),
         out_shape=(
@@ -427,9 +447,6 @@
         cost_estimate=cost(1000, 1000),
         name="local_samples",
     )(phases[None], record, own0)
-    own, z8 = lax.optimization_barrier((own, z8))
-    z12 = swap(z8, 4)
-    others = [z4, z12, z8]
     side, near = swap(own, 2), swap(own, 1)
     others, rounded, sel = lax.optimization_barrier((others, rounded, sel))
     far = jnp.concatenate(others, axis=0)
@@ -502,7 +519,8 @@
         scratch_shapes=[
             pltpu.VMEM((steps, cols), F32),
             pltpu.VMEM((3 * modes_r, cols), BF16),
-            pltpu.SemaphoreType.DMA((4,)),
+            pltpu.VMEM((3 * modes_r, cols), BF16),
+            pltpu.SemaphoreType.DMA((8,)),
         ],
         compiler_params=limit(16),
         cost_estimate=cost(1000000000, 9000000),

time: 30.8 us -> 30.4 us (0.987)
  starting transfers between devices: 12.6 us -> 11.1 us
  waiting for transfers between devices: 6.22 us -> 7.25 us
    ppermute x9, starting transfers between devices: 11 us -> 9.5 us  [swap(): return lax.ppermute(value, 'tm', [(i, i ^ bit) for i in range(groups)])]
    ppermute x9, waiting for transfers between devices: 2.67 us -> 3.68 us  [swap(): return lax.ppermute(value, 'tm', [(i, i ^ bit) for i in range(groups)])]
where the time goes in v2:
time: 30.4 us; the launch traced here: 30.3 us
  Pallas kernels  11.8 us (39%)
  starting transfers between devices  11.1 us (37%)
  waiting for transfers between devices  7.25 us (24%)
    ppermute x9, starting transfers between devices, swap(): return lax.ppermute(value, 'tm', [(i, i ^ bit) for i in range(groups)])  9.5 us
    pallas_call x1, Pallas kernels, body(): pl.pallas_call(solve_kernel, out_shape=shape(steps, cols), in_specs=[vmem...  6.09 us
    ppermute x9, waiting for transfers between devices, swap(): return lax.ppermute(value, 'tm', [(i, i ^ bit) for i in range(groups)])  3.68 us
    ppermute x1, waiting for transfers between devices, body(): other = lax.ppermute(w, 'space', [(i, i ^ distance) for i in range(spaces)])  3.57 us
    pallas_call x1, Pallas kernels, body(): pl.pallas_call(functools.partial(cross_kernel, points, size0), out_shape=...  1.85 us
    ppermute x1, starting transfers between devices, body(): other = lax.ppermute(w, 'space', [(i, i ^ distance) for i in range(spaces)])  1.57 us
    pallas_call x1, Pallas kernels, body(): pl.pallas_call(functools.partial(gram_kernel, points, size0), out_shape=(...  1.11 us
    pallas_call x1, Pallas kernels, body(): pl.pallas_call(functools.partial(slab_kernel, strides[0]), out_shape=shap...  1.09 us
  transfers between devices with their start and end apart: 10, of which 4 were waited for; matrix products, arithmetic and copies ran while one was open for 0% of the time, Pallas kernels for 8%

profile of v2, /device:TPU:0, one launch (start us, length us, event | category | flops | bytes accessed | tf_op | source)
XLA Modules:
  0.0 30.3 jit_solution(17297966423237367344)
XLA Ops:
  0.0 0.0 copy-start
  0.0 1.1 %sample_slabs.1.slab_ref = f32[16,4096]{1,0:T(8,128)S(1)} custom-call(f32[192,4096]{1,0:T(8,128)} %x_ref.3), custom_call_target="tpu_custom_call" | custom-call | bytes 200000 | tf_op jit(solution)/shard_map/sample_slabs/pallas_call | solution.py:415
  1.1 0.0 copy-done.3
  1.1 0.3 first_samples.1.own0_ref
  1.4 4.1 %collective-permute-start.2 = (bf16[96,128]{1,0:T(8,128)(2,1)S(1)}, bf16[96,128]{1,0:T(8,128)(2,1)S(1)}, u32[]{:S(2)}, u32[]{:S(2)}) collective-permute-start(bf16[96,128]{1,0:T(8,128)(2,1)S(1)} %first_samples.1.own0_ref), channel_id=1, source_target_pairs={{0,8},{1,9},{2,10},{3,11},{4,12},{5,13},{6,14},{7,15},{8,0},{9,1},... | collective-permute-start | bytes 73736 | tf_op jit(solution)/shard_map/ppermute | solution.py:409
  5.5 1.3 %collective-permute-start.1 = (bf16[96,128]{1,0:T(8,128)(2,1)S(1)}, bf16[96,128]{1,0:T(8,128)(2,1)S(1)}, u32[]{:S(2)}, u32[]{:S(2)}) collective-permute-start(bf16[96,128]{1,0:T(8,128)(2,1)S(1)} %first_samples.1.own0_ref), channel_id=1, source_target_pairs={{0,12},{1,13},{2,14},{3,15},{4,8},{5,9},{6,10},{7,11},{8,4},{9,5},... | collective-permute-start | bytes 73736 | tf_op jit(solution)/shard_map/ppermute | solution.py:409
  6.8 0.2 collective-permute-start
  7.1 0.0 copy-done
  7.1 0.6 %local_samples.1 = (bf16[192,4096]{1,0:T(8,128)(2,1)S(1)}, bf16[48,4096]{1,0:T(8,128)(2,1)S(1)}, bf16[480,128]{1,0:T(8,128)(2,1)S(1)}) custom-call(s32[1,21]{1,0:T(1,128)S(1)} %bitcast.3, f32[192,4096]{1,0:T(8,128)S(1)} %copy-done, bf16[96,128]{1,0:T(8,128)(2,1)S(1)} %first_samples.1.own0_ref), custom_call_target="tpu_custom_call" | custom-call | flops 1000 | bytes 1000 | tf_op jit(solution)/shard_map/local_samples/pallas_call | solution.py:438
  7.7 1.6 %collective-permute-start.6 = (bf16[480,128]{1,0:T(8,128)(2,1)S(1)}, bf16[480,128]{1,0:T(8,128)(2,1)S(1)}, u32[]{:S(2)}, u32[]{:S(2)}) collective-permute-start(bf16[480,128]{1,0:T(8,128)(2,1)S(1)} %get-tuple-element.42.refs_0_), channel_id=1, source_target_pairs={{0,2},{1,3},{2,0},{3,1},{4,6},{5,7},{6,4},{7,5},{8,10},{9,11},{10,... | collective-permute-start | bytes 368648 | tf_op jit(solution)/shard_map/ppermute | solution.py:409
  9.3 0.0 collective-permute-done.2
  9.3 1.8 %collective-permute-done.1 = bf16[96,128]{1,0:T(8,128)(2,1)S(1)} collective-permute-done((bf16[96,128]{1,0:T(8,128)(2,1)S(1)}, bf16[96,128]{1,0:T(8,128)(2,1)S(1)}, u32[]{:S(2)}, u32[]{:S(2)}) %collective-permute-start.1) | collective-permute-done | bytes 24608 | tf_op jit(solution)/shard_map/ppermute | solution.py:409
  11.1 0.0 collective-permute-done
  11.1 0.1 collective-permute-start.4
  11.2 1.6 %collective-permute-start.3 = (bf16[288,128]{1,0:T(8,128)(2,1)S(1)}, bf16[288,128]{1,0:T(8,128)(2,1)S(1)}, u32[]{:S(2)}, u32[]{:S(2)}) collective-permute-start(bf16[288,128]{1,0:T(8,128)(2,1)S(1)} %constant_dynamic-update-slice_fusion.refs_4_), channel_id=1, source_target_pairs={{0,2},{1,3},{2,0},{3,1},{4,6},{5,7},{6,4},{7,5},{8,10},{9,11},{10,... | collective-permute-start | bytes 221192 | tf_op jit(solution)/shard_map/ppermute | solution.py:409
  12.8 0.2 collective-permute-start.7
  13.0 0.0 copy-done.2
  13.0 0.0 copy-done.1
  13.0 0.8 %chosen_modes.1 = (f32[3,32,48]{2,1,0:T(8,128)S(1)}, f32[96,144]{1,0:T(8,128)S(1)}, f32[32,192]{1,0:T(8,128)S(1)}) custom-call(s32[1,21]{1,0:T(1,128)S(1)} %bitcast.4, f32[21,48,48]{2,1,0:T(8,128)S(1)} %copy-done.1, s32[21,32]{1,0:T(8,128)S(1)} %copy-done.2), custom_call_target="tpu_custom_call" | custom-call | flops 1000 | bytes 1000 | tf_op jit(solution)/shard_map/chosen_modes/pallas_call | solution.py:455
  13.8 0.0 collective-permute-done.6.refs_1_
  13.8 0.4 %collective-permute-start.8 = (bf16[480,128]{1,0:T(8,128)(2,1)S(1)}, bf16[480,128]{1,0:T(8,128)(2,1)S(1)}, u32[]{:S(2)}, u32[]{:S(2)}) collective-permute-start(bf16[480,128]{1,0:T(8,128)(2,1)S(1)} %collective-permute-done.6.refs_1_), channel_id=1, source_target_pairs={{0,1},{1,0},{2,3},{3,2},{4,5},{5,4},{6,7},{7,6},{8,9},{9,8},{10,11... | collective-permute-start | bytes 368648 | tf_op jit(solution)/shard_map/ppermute | solution.py:409
  14.2 0.0 collective-permute-done.4.refs_6_.far2_ref
  14.2 1.7 %collective-permute-done.3.refs_5_ = bf16[288,128]{1,0:T(8,128)(2,1)S(1)} collective-permute-done((bf16[288,128]{1,0:T(8,128)(2,1)S(1)}, bf16[288,128]{1,0:T(8,128)(2,1)S(1)}, u32[]{:S(2)}, u32[]{:S(2)}) %collective-permute-start.3) | collective-permute-done | bytes 73760 | tf_op jit(solution)/shard_map/ppermute | solution.py:409
  15.9 0.0 collective-permute-start.5
  15.9 0.0 collective-permute-done.7.refs_2_
  15.9 0.0 collective-permute-done.8.refs_3_.near3_ref
  15.9 1.1 %level_1_gram.1 = (f32[48,48]{1,0:T(8,128)S(1)}, bf16[128,4096]{1,0:T(8,128)(2,1)S(1)}) custom-call(bf16[48,4096]{1,0:T(8,128)(2,1)S(1)} %get-tuple-element.41.sel_ref, bf16[480,128]{1,0:T(8,128)(2,1)S(1)} %get-tuple-element.42.refs_0_, bf16[480,128]{1,0:T(8,128)(2,1)S(1)} %collective-permute-done.6.refs_1_, ...), custom_call_target="tpu_custom_call" | custom-call | flops 1000 | bytes 1000 | tf_op jit(solution)/shard_map/level_1_gram/pallas_call | solution.py:480
  17.0 0.1 collective-permute-done.5.far3_ref
  17.2 1.9 %cross_products.1 = (f32[96,256]{1,0:T(8,128)S(1)}, bf16[16,4096]{1,0:T(8,128)(2,1)S(1)}) custom-call(bf16[192,4096]{1,0:T(8,128)(2,1)S(1)} %get-tuple-element.34.round_ref, bf16[128,4096]{1,0:T(8,128)(2,1)S(1)} %get-tuple-element.51.early_ref, f32[48,48]{1,0:T(8,128)S(1)} %get-tuple-element.52.gram_ref, f32[96,144]{1,0:T(8,128)S(1)} %get-tuple-element.53.bd_ref, ...), custom_call_target="tpu_custom_call" | custom-call | flops 1000000000 | bytes 3000000 | tf_op jit(solution)/shard_map/cross_products/pallas_call | solution.py:493
  19.0 1.6 %collective-permute-start.9 = (f32[96,256]{1,0:T(8,128)S(1)}, f32[96,256]{1,0:T(8,128)S(1)}, u32[]{:S(2)}, u32[]{:S(2)}) collective-permute-start(f32[96,256]{1,0:T(8,128)S(1)} %get-tuple-element.56.w_ref), channel_id=1, source_target_pairs={{0,16},{16,0},{1,17},{17,1},{2,18},{18,2},{3,19},{19,3},{4,20},{20... | collective-permute-start | bytes 294920 | tf_op jit(solution)/shard_map/ppermute | solution.py:509
  20.6 3.6 %collective-permute-done.9.got_ref = f32[96,256]{1,0:T(8,128)S(1)} collective-permute-done((f32[96,256]{1,0:T(8,128)S(1)}, f32[96,256]{1,0:T(8,128)S(1)}, u32[]{:S(2)}, u32[]{:S(2)}) %collective-permute-start.9) | collective-permute-done | bytes 98336 | tf_op jit(solution)/shard_map/ppermute | solution.py:509
  24.2 6.1 %remove_slow.1 = f32[192,4096]{1,0:T(8,128)} custom-call(f32[96,256]{1,0:T(8,128)S(1)} %get-tuple-element.56.w_ref, f32[96,256]{1,0:T(8,128)S(1)} %collective-permute-done.9.got_ref, f32[3,32,48]{2,1,0:T(8,128)S(1)} %get-tuple-element.57.bt_ref, f32[192,4096]{1,0:T(8,128)S(1)} %copy-done, bf16[128,4096]{1,0:T(8,128)(2,1)S(1)} %get-tuple-element.51.early_ref, ...), custom_call_target="tpu_custom_call" | custom-call | flops 1000000000 | bytes 9000000 | tf_op jit(solution)/shard_map/remove_slow/pallas_call | solution.py:514
  (6 shorter events, 0.0 us)
Async XLA Ops:
  0.0 7.1 %copy-start = (f32[192,4096]{1,0:T(8,128)S(1)}, f32[192,4096]{1,0:T(8,128)}, u32[]{:S(2)}) copy-start(f32[192,4096]{1,0:T(8,128)} %x_ref.3) | copy-start | bytes 9437188
  0.0 1.1 %copy-start.3 = (s32[21]{0:T(128)S(1)}, s32[21]{0:T(128)}, u32[]{:S(2)}) copy-start(s32[21]{0:T(128)} %param.7) | copy-start | bytes 256
  0.0 13.0 %copy-start.2 = (s32[21,32]{1,0:T(8,128)S(1)}, s32[21,32]{1,0:T(8,128)}, u32[]{:S(2)}) copy-start(s32[21,32]{1,0:T(8,128)} %picks_ref.1) | copy-start | bytes 8068
  0.0 13.0 %copy-start.1 = (f32[21,48,48]{2,1,0:T(8,128)S(1)}, f32[21,48,48]{2,1,0:T(8,128)}, u32[]{:S(2)}) copy-start(f32[21,48,48]{2,1,0:T(8,128)} %basis_hbm.1) | copy-start | bytes 580612
  1.4 7.9 %collective-permute-start.2 = (bf16[96,128]{1,0:T(8,128)(2,1)S(1)}, bf16[96,128]{1,0:T(8,128)(2,1)S(1)}, u32[]{:S(2)}, u32[]{:S(2)}) collective-permute-start(bf16[96,128]{1,0:T(8,128)(2,1)S(1)} %first_samples.1.own0_ref), channel_id=1, source_target_pairs={{0,8},{1,9},{2,10},{3,11},{4,12},{5,13},{6,14},{7,15},{8,0},{9,1},... | collective-permute-start | bytes 73736 | tf_op jit(solution)/shard_map/ppermute | solution.py:409
  5.5 5.6 %collective-permute-start.1 = (bf16[96,128]{1,0:T(8,128)(2,1)S(1)}, bf16[96,128]{1,0:T(8,128)(2,1)S(1)}, u32[]{:S(2)}, u32[]{:S(2)}) collective-permute-start(bf16[96,128]{1,0:T(8,128)(2,1)S(1)} %first_samples.1.own0_ref), channel_id=1, source_target_pairs={{0,12},{1,13},{2,14},{3,15},{4,8},{5,9},{6,10},{7,11},{8,4},{9,5},... | collective-permute-start | bytes 73736 | tf_op jit(solution)/shard_map/ppermute | solution.py:409
  6.8 4.3 %collective-permute-start = (bf16[96,128]{1,0:T(8,128)(2,1)S(1)}, bf16[96,128]{1,0:T(8,128)(2,1)S(1)}, u32[]{:S(2)}, u32[]{:S(2)}) collective-permute-start(bf16[96,128]{1,0:T(8,128)(2,1)S(1)} %first_samples.1.own0_ref), channel_id=1, source_target_pairs={{0,4},{1,5},{2,6},{3,7},{4,0},{5,1},{6,2},{7,3},{8,12},{9,13},{10,... | collective-permute-start | bytes 73736 | tf_op jit(solution)/shard_map/ppermute | solution.py:409
  7.7 6.1 %collective-permute-start.6 = (bf16[480,128]{1,0:T(8,128)(2,1)S(1)}, bf16[480,128]{1,0:T(8,128)(2,1)S(1)}, u32[]{:S(2)}, u32[]{:S(2)}) collective-permute-start(bf16[480,128]{1,0:T(8,128)(2,1)S(1)} %get-tuple-element.42.refs_0_), channel_id=1, source_target_pairs={{0,2},{1,3},{2,0},{3,1},{4,6},{5,7},{6,4},{7,5},{8,10},{9,11},{10,... | collective-permute-start | bytes 368648 | tf_op jit(solution)/shard_map/ppermute | solution.py:409
  11.1 3.1 %collective-permute-start.4 = (bf16[288,128]{1,0:T(8,128)(2,1)S(1)}, bf16[288,128]{1,0:T(8,128)(2,1)S(1)}, u32[]{:S(2)}, u32[]{:S(2)}) collective-permute-start(bf16[288,128]{1,0:T(8,128)(2,1)S(1)} %constant_dynamic-update-slice_fusion.refs_4_), channel_id=1, source_target_pairs={{0,1},{1,0},{2,3},{3,2},{4,5},{5,4},{6,7},{7,6},{8,9},{9,8},{10,11... | collective-permute-start | bytes 221192 | tf_op jit(solution)/shard_map/ppermute | solution.py:409
  11.2 4.7 %collective-permute-start.3 = (bf16[288,128]{1,0:T(8,128)(2,1)S(1)}, bf16[288,128]{1,0:T(8,128)(2,1)S(1)}, u32[]{:S(2)}, u32[]{:S(2)}) collective-permute-start(bf16[288,128]{1,0:T(8,128)(2,1)S(1)} %constant_dynamic-update-slice_fusion.refs_4_), channel_id=1, source_target_pairs={{0,2},{1,3},{2,0},{3,1},{4,6},{5,7},{6,4},{7,5},{8,10},{9,11},{10,... | collective-permute-start | bytes 221192 | tf_op jit(solution)/shard_map/ppermute | solution.py:409
  12.8 3.1 %collective-permute-start.7 = (bf16[480,128]{1,0:T(8,128)(2,1)S(1)}, bf16[480,128]{1,0:T(8,128)(2,1)S(1)}, u32[]{:S(2)}, u32[]{:S(2)}) collective-permute-start(bf16[480,128]{1,0:T(8,128)(2,1)S(1)} %get-tuple-element.42.refs_0_), channel_id=1, source_target_pairs={{0,1},{1,0},{2,3},{3,2},{4,5},{5,4},{6,7},{7,6},{8,9},{9,8},{10,11... | collective-permute-start | bytes 368648 | tf_op jit(solution)/shard_map/ppermute | solution.py:409
  13.8 2.1 %collective-permute-start.8 = (bf16[480,128]{1,0:T(8,128)(2,1)S(1)}, bf16[480,128]{1,0:T(8,128)(2,1)S(1)}, u32[]{:S(2)}, u32[]{:S(2)}) collective-permute-start(bf16[480,128]{1,0:T(8,128)(2,1)S(1)} %collective-permute-done.6.refs_1_), channel_id=1, source_target_pairs={{0,1},{1,0},{2,3},{3,2},{4,5},{5,4},{6,7},{7,6},{8,9},{9,8},{10,11... | collective-permute-start | bytes 368648 | tf_op jit(solution)/shard_map/ppermute | solution.py:409
  15.9 1.3 %collective-permute-start.5 = (bf16[288,128]{1,0:T(8,128)(2,1)S(1)}, bf16[288,128]{1,0:T(8,128)(2,1)S(1)}, u32[]{:S(2)}, u32[]{:S(2)}) collective-permute-start(bf16[288,128]{1,0:T(8,128)(2,1)S(1)} %collective-permute-done.3.refs_5_), channel_id=1, source_target_pairs={{0,1},{1,0},{2,3},{3,2},{4,5},{5,4},{6,7},{7,6},{8,9},{9,8},{10,11... | collective-permute-start | bytes 221192 | tf_op jit(solution)/shard_map/ppermute | solution.py:409
  19.0 5.1 %collective-permute-start.9 = (f32[96,256]{1,0:T(8,128)S(1)}, f32[96,256]{1,0:T(8,128)S(1)}, u32[]{:S(2)}, u32[]{:S(2)}) collective-permute-start(f32[96,256]{1,0:T(8,128)S(1)} %get-tuple-element.56.w_ref), channel_id=1, source_target_pairs={{0,16},{16,0},{1,17},{17,1},{2,18},{18,2},{3,19},{19,3},{4,20},{20... | collective-permute-start | bytes 294920 | tf_op jit(solution)/shard_map/ppermute | solution.py:509

commit v3 on v1

--- a/solution.py
+++ b/solution.py
@@ -37,6 +37,24 @@
 def split2(x):
     high = x.astype(BF16)
     return high, (x - high.astype(F32)).astype(BF16)
+
+
+def split3(x):
+    high = x.astype(BF16)
+    rest = x - high.astype(F32)
+    middle = rest.astype(BF16)
+    return high, middle, (rest - middle.astype(F32)).astype(BF16)
+
+
+def dot_six(a, b):
+    m = a.shape[0]
+    a0, a1, a2 = split3(a)
+    b0, b1, b2 = split3(b)
+    p0 = dot_nn(jnp.concatenate([a0, a1, a2], axis=0), b0)
+    p1 = dot_nn(jnp.concatenate([a0, a1], axis=0), b1)
+    p2 = dot_nn(a0, b2)
+    small = (p0[2 * m:3 * m] + p1[m:2 * m]) + p2
+    return (small + (p0[m:2 * m] + p1[0:m])) + p0[0:m]
 
 
 def iota(shape, axis):
@@ -58,7 +76,7 @@
         for i in range(sems.shape[0])
     ]
     for copy in copies:
-        copy.start()
+        copy.start(priority=1)
     rows, cols = slab_ref.shape
     used = size * sems.shape[0]
     slab_ref[used:rows] = jnp.zeros((rows - used, cols), F32)
@@ -199,7 +217,7 @@
     s = jnp.concatenate([s0, early_ref[first:]], axis=0)
     cross = dot_nt(s, jnp.concatenate([round_ref[...], s0], axis=0)) * (1.0 / points)
     b0, b1 = bd_ref[0:r, 0:count], bd_ref[r:2 * r, count:2 * count]
-    wx = dot_nn(bd_ref[...], cross[:, 0:steps], HI)
+    wx = dot_six(bd_ref[...], cross[:, 0:steps])
     g0 = dot_nn(bd_ref[0:2 * r, 0:2 * count], cross[0:2 * count, steps:steps + count], HI)
     g1 = dot_nn(b1, gram_ref[...], HI)
     wy = dot_nt(b0, g0, HI)
@@ -281,8 +299,8 @@
                 tiles[g][t] = tile
         if k + 4 < groups * ROWS:
             cols = [[along_lanes(tiles[g][at], base + k + 4 + j) for g in range(groups)] for j in four]
-        if beside is not None:
-            beside(k // 4)
+        if beside is not None and k % 8 == 0:
+            beside(k // 8)
     return tiles
 
 
@@ -313,15 +331,20 @@
         return jnp.where(iota((r, width), 0) + base == iota((r, width), 1), EPS, 0.0)
 
     at1, at2 = steps, steps + r
+    assert at1 // LANES == (at2 + r - 1) // LANES
     a0 = w[0:r]
-    k0 = jnp.concatenate([w[2 * r:3 * r, at1:at1 + r], jnp.zeros((r, LANES - r), F32)], axis=1)
-    k0 = k0 + eye_at(0, LANES)
-    solved = eliminate(to_tiles(jnp.concatenate([a0, k0], axis=1)), lanes // LANES, 0)
+    tile1, lane1 = at1 // LANES, at1 % LANES
+    tile2, lane2 = at2 // LANES, at2 % LANES
+    k0 = w[2 * r:3 * r] + eye_at(at1, lanes)
+    solved = eliminate(
+        to_tiles(jnp.concatenate([a0, k0[:, tile1 * LANES:(tile1 + 1) * LANES]], axis=1)),
+        lanes // LANES, lane1,
+    )
     v0 = from_tiles([row[0:lanes // LANES] for row in solved])
     t0 = a0 + EPS * v0
     a1 = w[r:2 * r] - dot_tn(v0[:, at1:at1 + r], t0, HI)
     part2 = w[2 * r:3 * r] - dot_tn(v0[:, at2:at2 + r], t0, HI)
-    v1 = from_tiles(eliminate(to_tiles(a1 + eye_at(at1, lanes)), at1 // LANES, at1 % LANES))
+    v1 = from_tiles(eliminate(to_tiles(a1 + eye_at(at1, lanes)), tile1, lane1))
     t1 = a1 + EPS * v1
     a2 = part2 - dot_tn(v1[:, at2:at2 + r], t1, HI)
     v0 = v0 - dot_nn(v0[:, at1:at1 + r], v1, HI)
@@ -333,7 +356,7 @@
         [-dot_tn(v0[:, at2:at2 + r], b0, HI), -dot_tn(v1[:, at2:at2 + r], b1, HI), b2], axis=1
     )
     turn = jnp.concatenate(split2(turn), axis=0)
-    parts = r // 4
+    parts = r // 8
     wide = cols // parts
 
     def beside(p):
@@ -349,7 +372,6 @@
         z_ref[r:2 * r, at] = high
         z_ref[2 * r:3 * r, at] = low
 
-    tile2, lane2 = at2 // LANES, at2 % LANES
     v2 = from_tiles(eliminate(to_tiles(a2 + eye_at(at2, lanes)), tile2, lane2, beside))
     high = v2[:, 0:steps].astype(BF16).astype(F32)
     late = jnp.concatenate([high, v2[:, 0:steps] - high, high], axis=0).T.astype(BF16)
@@ -414,7 +436,8 @@
         name="first_samples",
     )(phases[None], slab)
 
-    z8, z4 = [swap(own0, bit) for bit in (8, 4)]
+    z8, z12, z4 = [swap(own0, bit) for bit in (8, 12, 4)]
+    others = [z4, z12, z8]
     rounded, sel, own = pl.pallas_call(
         functools.partial(local_kernel, strides),
         out_shape=(
@@ -427,9 +450,6 @@
         cost_estimate=cost(1000, 1000),
         name="local_samples",
     )(phases[None], record, own0)
-    own, z8 = lax.optimization_barrier((own, z8))
-    z12 = swap(z8, 4)
-    others = [z4, z12, z8]
     side, near = swap(own, 2), swap(own, 1)
     others, rounded, sel = lax.optimization_barrier((others, rounded, sel))
     far = jnp.concatenate(others, axis=0)
@@ -502,7 +522,7 @@
         scratch_shapes=[
             pltpu.VMEM((steps, cols), F32),
             pltpu.VMEM((3 * modes_r, cols), BF16),
-            pltpu.SemaphoreType.DMA((4,)),
+            pltpu.SemaphoreType.DMA((8,)),
         ],
         compiler_params=limit(16),
         cost_estimate=cost(1000000000, 9000000),

time: 30.8 us -> 30.2 us (0.981)
  starting transfers between devices: 12.6 us -> 11.1 us
  waiting for transfers between devices: 6.22 us -> 7.25 us
    ppermute x9, starting transfers between devices: 11 us -> 9.5 us  [swap(): return lax.ppermute(value, 'tm', [(i, i ^ bit) for i in range(groups)])]
    ppermute x9, waiting for transfers between devices: 2.67 us -> 3.68 us  [swap(): return lax.ppermute(value, 'tm', [(i, i ^ bit) for i in range(groups)])]
where the time goes in v3:
time: 30.2 us; the launch traced here: 30 us
  Pallas kernels  11.6 us (38%)
  starting transfers between devices  11.1 us (37%)
  waiting for transfers between devices  7.25 us (24%)
    ppermute x9, starting transfers between devices, swap(): return lax.ppermute(value, 'tm', [(i, i ^ bit) for i in range(groups)])  9.5 us
    pallas_call x1, Pallas kernels, body(): pl.pallas_call(solve_kernel, out_shape=shape(steps, cols), in_specs=[vmem...  5.85 us
    ppermute x9, waiting for transfers between devices, swap(): return lax.ppermute(value, 'tm', [(i, i ^ bit) for i in range(groups)])  3.68 us
    ppermute x1, waiting for transfers between devices, body(): other = lax.ppermute(w, 'space', [(i, i ^ distance) for i in range(spaces)])  3.57 us
    pallas_call x1, Pallas kernels, body(): pl.pallas_call(functools.partial(cross_kernel, points, size0), out_shape=...  1.85 us
    ppermute x1, starting transfers between devices, body(): other = lax.ppermute(w, 'space', [(i, i ^ distance) for i in range(spaces)])  1.57 us
    pallas_call x1, Pallas kernels, body(): pl.pallas_call(functools.partial(gram_kernel, points, size0), out_shape=(...  1.11 us
    pallas_call x1, Pallas kernels, body(): pl.pallas_call(functools.partial(slab_kernel, strides[0]), out_shape=shap...  1.09 us
  transfers between devices with their start and end apart: 10, of which 4 were waited for; matrix products, arithmetic and copies ran while one was open for 0% of the time, Pallas kernels for 8%

profile of v3, /device:TPU:0, one launch (start us, length us, event | category | flops | bytes accessed | tf_op | source)
XLA Modules:
  0.0 30.0 jit_solution(5455471136442668437)
XLA Ops:
  0.0 0.0 copy-start
  0.0 1.1 %sample_slabs.1.slab_ref = f32[16,4096]{1,0:T(8,128)S(1)} custom-call(f32[192,4096]{1,0:T(8,128)} %x_ref.3), custom_call_target="tpu_custom_call" | custom-call | bytes 200000 | tf_op jit(solution)/shard_map/sample_slabs/pallas_call | solution.py:418
  1.1 0.0 copy-done.3
  1.1 0.3 first_samples.1.own0_ref
  1.4 4.1 %collective-permute-start.2 = (bf16[96,128]{1,0:T(8,128)(2,1)S(1)}, bf16[96,128]{1,0:T(8,128)(2,1)S(1)}, u32[]{:S(2)}, u32[]{:S(2)}) collective-permute-start(bf16[96,128]{1,0:T(8,128)(2,1)S(1)} %first_samples.1.own0_ref), channel_id=1, source_target_pairs={{0,8},{1,9},{2,10},{3,11},{4,12},{5,13},{6,14},{7,15},{8,0},{9,1},... | collective-permute-start | bytes 73736 | tf_op jit(solution)/shard_map/ppermute | solution.py:412
  5.5 1.3 %collective-permute-start.1 = (bf16[96,128]{1,0:T(8,128)(2,1)S(1)}, bf16[96,128]{1,0:T(8,128)(2,1)S(1)}, u32[]{:S(2)}, u32[]{:S(2)}) collective-permute-start(bf16[96,128]{1,0:T(8,128)(2,1)S(1)} %first_samples.1.own0_ref), channel_id=1, source_target_pairs={{0,12},{1,13},{2,14},{3,15},{4,8},{5,9},{6,10},{7,11},{8,4},{9,5},... | collective-permute-start | bytes 73736 | tf_op jit(solution)/shard_map/ppermute | solution.py:412
  6.8 0.2 collective-permute-start
  7.1 0.0 copy-done
  7.1 0.6 %local_samples.1 = (bf16[192,4096]{1,0:T(8,128)(2,1)S(1)}, bf16[48,4096]{1,0:T(8,128)(2,1)S(1)}, bf16[480,128]{1,0:T(8,128)(2,1)S(1)}) custom-call(s32[1,21]{1,0:T(1,128)S(1)} %bitcast.3, f32[192,4096]{1,0:T(8,128)S(1)} %copy-done, bf16[96,128]{1,0:T(8,128)(2,1)S(1)} %first_samples.1.own0_ref), custom_call_target="tpu_custom_call" | custom-call | flops 1000 | bytes 1000 | tf_op jit(solution)/shard_map/local_samples/pallas_call | solution.py:441
  7.7 1.6 %collective-permute-start.6 = (bf16[480,128]{1,0:T(8,128)(2,1)S(1)}, bf16[480,128]{1,0:T(8,128)(2,1)S(1)}, u32[]{:S(2)}, u32[]{:S(2)}) collective-permute-start(bf16[480,128]{1,0:T(8,128)(2,1)S(1)} %get-tuple-element.42.refs_0_), channel_id=1, source_target_pairs={{0,2},{1,3},{2,0},{3,1},{4,6},{5,7},{6,4},{7,5},{8,10},{9,11},{10,... | collective-permute-start | bytes 368648 | tf_op jit(solution)/shard_map/ppermute | solution.py:412
  9.3 0.0 collective-permute-done.2
  9.3 1.8 %collective-permute-done.1 = bf16[96,128]{1,0:T(8,128)(2,1)S(1)} collective-permute-done((bf16[96,128]{1,0:T(8,128)(2,1)S(1)}, bf16[96,128]{1,0:T(8,128)(2,1)S(1)}, u32[]{:S(2)}, u32[]{:S(2)}) %collective-permute-start.1) | collective-permute-done | bytes 24608 | tf_op jit(solution)/shard_map/ppermute | solution.py:412
  11.1 0.0 collective-permute-done
  11.1 0.1 collective-permute-start.4
  11.2 1.6 %collective-permute-start.3 = (bf16[288,128]{1,0:T(8,128)(2,1)S(1)}, bf16[288,128]{1,0:T(8,128)(2,1)S(1)}, u32[]{:S(2)}, u32[]{:S(2)}) collective-permute-start(bf16[288,128]{1,0:T(8,128)(2,1)S(1)} %constant_dynamic-update-slice_fusion.refs_4_), channel_id=1, source_target_pairs={{0,2},{1,3},{2,0},{3,1},{4,6},{5,7},{6,4},{7,5},{8,10},{9,11},{10,... | collective-permute-start | bytes 221192 | tf_op jit(solution)/shard_map/ppermute | solution.py:412
  12.8 0.2 collective-permute-start.7
  13.0 0.0 copy-done.2
  13.0 0.0 copy-done.1
  13.0 0.8 %chosen_modes.1 = (f32[3,32,48]{2,1,0:T(8,128)S(1)}, f32[96,144]{1,0:T(8,128)S(1)}, f32[32,192]{1,0:T(8,128)S(1)}) custom-call(s32[1,21]{1,0:T(1,128)S(1)} %bitcast.4, f32[21,48,48]{2,1,0:T(8,128)S(1)} %copy-done.1, s32[21,32]{1,0:T(8,128)S(1)} %copy-done.2), custom_call_target="tpu_custom_call" | custom-call | flops 1000 | bytes 1000 | tf_op jit(solution)/shard_map/chosen_modes/pallas_call | solution.py:458
  13.8 0.0 collective-permute-done.6.refs_1_
  13.8 0.4 %collective-permute-start.8 = (bf16[480,128]{1,0:T(8,128)(2,1)S(1)}, bf16[480,128]{1,0:T(8,128)(2,1)S(1)}, u32[]{:S(2)}, u32[]{:S(2)}) collective-permute-start(bf16[480,128]{1,0:T(8,128)(2,1)S(1)} %collective-permute-done.6.refs_1_), channel_id=1, source_target_pairs={{0,1},{1,0},{2,3},{3,2},{4,5},{5,4},{6,7},{7,6},{8,9},{9,8},{10,11... | collective-permute-start | bytes 368648 | tf_op jit(solution)/shard_map/ppermute | solution.py:412
  14.2 0.0 collective-permute-done.4.refs_6_.far2_ref
  14.2 1.7 %collective-permute-done.3.refs_5_ = bf16[288,128]{1,0:T(8,128)(2,1)S(1)} collective-permute-done((bf16[288,128]{1,0:T(8,128)(2,1)S(1)}, bf16[288,128]{1,0:T(8,128)(2,1)S(1)}, u32[]{:S(2)}, u32[]{:S(2)}) %collective-permute-start.3) | collective-permute-done | bytes 73760 | tf_op jit(solution)/shard_map/ppermute | solution.py:412
  15.9 0.0 collective-permute-start.5
  15.9 0.0 collective-permute-done.7.refs_2_
  15.9 0.0 collective-permute-done.8.refs_3_.near3_ref
  15.9 1.1 %level_1_gram.1 = (f32[48,48]{1,0:T(8,128)S(1)}, bf16[128,4096]{1,0:T(8,128)(2,1)S(1)}) custom-call(bf16[48,4096]{1,0:T(8,128)(2,1)S(1)} %get-tuple-element.41.sel_ref, bf16[480,128]{1,0:T(8,128)(2,1)S(1)} %get-tuple-element.42.refs_0_, bf16[480,128]{1,0:T(8,128)(2,1)S(1)} %collective-permute-done.6.refs_1_, ...), custom_call_target="tpu_custom_call" | custom-call | flops 1000 | bytes 1000 | tf_op jit(solution)/shard_map/level_1_gram/pallas_call | solution.py:483
  17.0 0.1 collective-permute-done.5.far3_ref
  17.2 1.9 %cross_products.1 = (f32[96,256]{1,0:T(8,128)S(1)}, bf16[16,4096]{1,0:T(8,128)(2,1)S(1)}) custom-call(bf16[192,4096]{1,0:T(8,128)(2,1)S(1)} %get-tuple-element.34.round_ref, bf16[128,4096]{1,0:T(8,128)(2,1)S(1)} %get-tuple-element.51.early_ref, f32[48,48]{1,0:T(8,128)S(1)} %get-tuple-element.52.gram_ref, f32[96,144]{1,0:T(8,128)S(1)} %get-tuple-element.53.bd_ref, ...), custom_call_target="tpu_custom_call" | custom-call | flops 1000000000 | bytes 3000000 | tf_op jit(solution)/shard_map/cross_products/pallas_call | solution.py:496
  19.0 1.6 %collective-permute-start.9 = (f32[96,256]{1,0:T(8,128)S(1)}, f32[96,256]{1,0:T(8,128)S(1)}, u32[]{:S(2)}, u32[]{:S(2)}) collective-permute-start(f32[96,256]{1,0:T(8,128)S(1)} %get-tuple-element.56.w_ref), channel_id=1, source_target_pairs={{0,16},{16,0},{1,17},{17,1},{2,18},{18,2},{3,19},{19,3},{4,20},{20... | collective-permute-start | bytes 294920 | tf_op jit(solution)/shard_map/ppermute | solution.py:512
  20.6 3.6 %collective-permute-done.9.got_ref = f32[96,256]{1,0:T(8,128)S(1)} collective-permute-done((f32[96,256]{1,0:T(8,128)S(1)}, f32[96,256]{1,0:T(8,128)S(1)}, u32[]{:S(2)}, u32[]{:S(2)}) %collective-permute-start.9) | collective-permute-done | bytes 98336 | tf_op jit(solution)/shard_map/ppermute | solution.py:512
  24.2 5.8 %remove_slow.1 = f32[192,4096]{1,0:T(8,128)} custom-call(f32[96,256]{1,0:T(8,128)S(1)} %get-tuple-element.56.w_ref, f32[96,256]{1,0:T(8,128)S(1)} %collective-permute-done.9.got_ref, f32[3,32,48]{2,1,0:T(8,128)S(1)} %get-tuple-element.57.bt_ref, f32[192,4096]{1,0:T(8,128)S(1)} %copy-done, bf16[128,4096]{1,0:T(8,128)(2,1)S(1)} %get-tuple-element.51.early_ref, ...), custom_call_target="tpu_custom_call" | custom-call | flops 1000000000 | bytes 9000000 | tf_op jit(solution)/shard_map/remove_slow/pallas_call | solution.py:517
  (6 shorter events, 0.0 us)
Async XLA Ops:
  0.0 7.1 %copy-start = (f32[192,4096]{1,0:T(8,128)S(1)}, f32[192,4096]{1,0:T(8,128)}, u32[]{:S(2)}) copy-start(f32[192,4096]{1,0:T(8,128)} %x_ref.3) | copy-start | bytes 9437188
  0.0 1.1 %copy-start.3 = (s32[21]{0:T(128)S(1)}, s32[21]{0:T(128)}, u32[]{:S(2)}) copy-start(s32[21]{0:T(128)} %param.7) | copy-start | bytes 256
  0.0 13.0 %copy-start.2 = (s32[21,32]{1,0:T(8,128)S(1)}, s32[21,32]{1,0:T(8,128)}, u32[]{:S(2)}) copy-start(s32[21,32]{1,0:T(8,128)} %picks_ref.1) | copy-start | bytes 8068
  0.0 13.0 %copy-start.1 = (f32[21,48,48]{2,1,0:T(8,128)S(1)}, f32[21,48,48]{2,1,0:T(8,128)}, u32[]{:S(2)}) copy-start(f32[21,48,48]{2,1,0:T(8,128)} %basis_hbm.1) | copy-start | bytes 580612
  1.4 7.9 %collective-permute-start.2 = (bf16[96,128]{1,0:T(8,128)(2,1)S(1)}, bf16[96,128]{1,0:T(8,128)(2,1)S(1)}, u32[]{:S(2)}, u32[]{:S(2)}) collective-permute-start(bf16[96,128]{1,0:T(8,128)(2,1)S(1)} %first_samples.1.own0_ref), channel_id=1, source_target_pairs={{0,8},{1,9},{2,10},{3,11},{4,12},{5,13},{6,14},{7,15},{8,0},{9,1},... | collective-permute-start | bytes 73736 | tf_op jit(solution)/shard_map/ppermute | solution.py:412
  5.5 5.6 %collective-permute-start.1 = (bf16[96,128]{1,0:T(8,128)(2,1)S(1)}, bf16[96,128]{1,0:T(8,128)(2,1)S(1)}, u32[]{:S(2)}, u32[]{:S(2)}) collective-permute-start(bf16[96,128]{1,0:T(8,128)(2,1)S(1)} %first_samples.1.own0_ref), channel_id=1, source_target_pairs={{0,12},{1,13},{2,14},{3,15},{4,8},{5,9},{6,10},{7,11},{8,4},{9,5},... | collective-permute-start | bytes 73736 | tf_op jit(solution)/shard_map/ppermute | solution.py:412
  6.8 4.3 %collective-permute-start = (bf16[96,128]{1,0:T(8,128)(2,1)S(1)}, bf16[96,128]{1,0:T(8,128)(2,1)S(1)}, u32[]{:S(2)}, u32[]{:S(2)}) collective-permute-start(bf16[96,128]{1,0:T(8,128)(2,1)S(1)} %first_samples.1.own0_ref), channel_id=1, source_target_pairs={{0,4},{1,5},{2,6},{3,7},{4,0},{5,1},{6,2},{7,3},{8,12},{9,13},{10,... | collective-permute-start | bytes 73736 | tf_op jit(solution)/shard_map/ppermute | solution.py:412
  7.7 6.1 %collective-permute-start.6 = (bf16[480,128]{1,0:T(8,128)(2,1)S(1)}, bf16[480,128]{1,0:T(8,128)(2,1)S(1)}, u32[]{:S(2)}, u32[]{:S(2)}) collective-permute-start(bf16[480,128]{1,0:T(8,128)(2,1)S(1)} %get-tuple-element.42.refs_0_), channel_id=1, source_target_pairs={{0,2},{1,3},{2,0},{3,1},{4,6},{5,7},{6,4},{7,5},{8,10},{9,11},{10,... | collective-permute-start | bytes 368648 | tf_op jit(solution)/shard_map/ppermute | solution.py:412
  11.1 3.1 %collective-permute-start.4 = (bf16[288,128]{1,0:T(8,128)(2,1)S(1)}, bf16[288,128]{1,0:T(8,128)(2,1)S(1)}, u32[]{:S(2)}, u32[]{:S(2)}) collective-permute-start(bf16[288,128]{1,0:T(8,128)(2,1)S(1)} %constant_dynamic-update-slice_fusion.refs_4_), channel_id=1, source_target_pairs={{0,1},{1,0},{2,3},{3,2},{4,5},{5,4},{6,7},{7,6},{8,9},{9,8},{10,11... | collective-permute-start | bytes 221192 | tf_op jit(solution)/shard_map/ppermute | solution.py:412
  11.2 4.7 %collective-permute-start.3 = (bf16[288,128]{1,0:T(8,128)(2,1)S(1)}, bf16[288,128]{1,0:T(8,128)(2,1)S(1)}, u32[]{:S(2)}, u32[]{:S(2)}) collective-permute-start(bf16[288,128]{1,0:T(8,128)(2,1)S(1)} %constant_dynamic-update-slice_fusion.refs_4_), channel_id=1, source_target_pairs={{0,2},{1,3},{2,0},{3,1},{4,6},{5,7},{6,4},{7,5},{8,10},{9,11},{10,... | collective-permute-start | bytes 221192 | tf_op jit(solution)/shard_map/ppermute | solution.py:412
  12.8 3.1 %collective-permute-start.7 = (bf16[480,128]{1,0:T(8,128)(2,1)S(1)}, bf16[480,128]{1,0:T(8,128)(2,1)S(1)}, u32[]{:S(2)}, u32[]{:S(2)}) collective-permute-start(bf16[480,128]{1,0:T(8,128)(2,1)S(1)} %get-tuple-element.42.refs_0_), channel_id=1, source_target_pairs={{0,1},{1,0},{2,3},{3,2},{4,5},{5,4},{6,7},{7,6},{8,9},{9,8},{10,11... | collective-permute-start | bytes 368648 | tf_op jit(solution)/shard_map/ppermute | solution.py:412
  13.8 2.1 %collective-permute-start.8 = (bf16[480,128]{1,0:T(8,128)(2,1)S(1)}, bf16[480,128]{1,0:T(8,128)(2,1)S(1)}, u32[]{:S(2)}, u32[]{:S(2)}) collective-permute-start(bf16[480,128]{1,0:T(8,128)(2,1)S(1)} %collective-permute-done.6.refs_1_), channel_id=1, source_target_pairs={{0,1},{1,0},{2,3},{3,2},{4,5},{5,4},{6,7},{7,6},{8,9},{9,8},{10,11... | collective-permute-start | bytes 368648 | tf_op jit(solution)/shard_map/ppermute | solution.py:412
  15.9 1.3 %collective-permute-start.5 = (bf16[288,128]{1,0:T(8,128)(2,1)S(1)}, bf16[288,128]{1,0:T(8,128)(2,1)S(1)}, u32[]{:S(2)}, u32[]{:S(2)}) collective-permute-start(bf16[288,128]{1,0:T(8,128)(2,1)S(1)} %collective-permute-done.3.refs_5_), channel_id=1, source_target_pairs={{0,1},{1,0},{2,3},{3,2},{4,5},{5,4},{6,7},{7,6},{8,9},{9,8},{10,11... | collective-permute-start | bytes 221192 | tf_op jit(solution)/shard_map/ppermute | solution.py:412
  19.0 5.1 %collective-permute-start.9 = (f32[96,256]{1,0:T(8,128)S(1)}, f32[96,256]{1,0:T(8,128)S(1)}, u32[]{:S(2)}, u32[]{:S(2)}) collective-permute-start(f32[96,256]{1,0:T(8,128)S(1)} %get-tuple-element.56.w_ref), channel_id=1, source_target_pairs={{0,16},{16,0},{1,17},{17,1},{2,18},{18,2},{3,19},{19,3},{4,20},{20... | collective-permute-start | bytes 294920 | tf_op jit(solution)/shard_map/ppermute | solution.py:512

commit v4 on v3

--- a/solution.py
+++ b/solution.py
@@ -276,6 +276,8 @@
     for k in range(0, groups * ROWS, 4):
         home, first = k // ROWS, k % ROWS
         m = inverse4(pivot)
+        if beside is not None:
+            beside(k // 4)
         if k + 4 < groups * ROWS:
             then, start = (k + 4) // ROWS, (k + 4) % ROWS
             left = [[along_rows(cols[j][then], start + i) for j in four] for i in four]
@@ -299,8 +301,6 @@
                 tiles[g][t] = tile
         if k + 4 < groups * ROWS:
             cols = [[along_lanes(tiles[g][at], base + k + 4 + j) for g in range(groups)] for j in four]
-        if beside is not None and k % 8 == 0:
-            beside(k // 8)
     return tiles
 
 
@@ -356,7 +356,7 @@
         [-dot_tn(v0[:, at2:at2 + r], b0, HI), -dot_tn(v1[:, at2:at2 + r], b1, HI), b2], axis=1
     )
     turn = jnp.concatenate(split2(turn), axis=0)
-    parts = r // 8
+    parts = r // 4
     wide = cols // parts
 
     def beside(p):

time: 30.2 us -> 30.1 us (level)
  no operation moved by 1% of the time
where the time goes in v4:
time: 30.1 us; the launch traced here: 30 us
  Pallas kernels  11.6 us (39%)
  starting transfers between devices  11.1 us (37%)
  waiting for transfers between devices  7.25 us (24%)
    ppermute x9, starting transfers between devices, swap(): return lax.ppermute(value, 'tm', [(i, i ^ bit) for i in range(groups)])  9.5 us
    pallas_call x1, Pallas kernels, body(): pl.pallas_call(solve_kernel, out_shape=shape(steps, cols), in_specs=[vmem...  5.84 us
    ppermute x9, waiting for transfers between devices, swap(): return lax.ppermute(value, 'tm', [(i, i ^ bit) for i in range(groups)])  3.68 us
    ppermute x1, waiting for transfers between devices, body(): other = lax.ppermute(w, 'space', [(i, i ^ distance) for i in range(spaces)])  3.57 us
    pallas_call x1, Pallas kernels, body(): pl.pallas_call(functools.partial(cross_kernel, points, size0), out_shape=...  1.85 us
    ppermute x1, starting transfers between devices, body(): other = lax.ppermute(w, 'space', [(i, i ^ distance) for i in range(spaces)])  1.57 us
    pallas_call x1, Pallas kernels, body(): pl.pallas_call(functools.partial(gram_kernel, points, size0), out_shape=(...  1.11 us
    pallas_call x1, Pallas kernels, body(): pl.pallas_call(functools.partial(slab_kernel, strides[0]), out_shape=shap...  1.09 us
  transfers between devices with their start and end apart: 10, of which 4 were waited for; matrix products, arithmetic and copies ran while one was open for 0% of the time, Pallas kernels for 8%

profile of v4, /device:TPU:0, one launch (start us, length us, event | category | flops | bytes accessed | tf_op | source)
XLA Modules:
  0.0 30.0 jit_solution(1158430174282937440)
XLA Ops:
  0.0 0.0 copy-start
  0.0 1.1 %sample_slabs.1.slab_ref = f32[16,4096]{1,0:T(8,128)S(1)} custom-call(f32[192,4096]{1,0:T(8,128)} %x_ref.3), custom_call_target="tpu_custom_call" | custom-call | bytes 200000 | tf_op jit(solution)/shard_map/sample_slabs/pallas_call | solution.py:418
  1.1 0.0 copy-done.3
  1.1 0.3 first_samples.1.own0_ref
  1.4 4.1 %collective-permute-start.2 = (bf16[96,128]{1,0:T(8,128)(2,1)S(1)}, bf16[96,128]{1,0:T(8,128)(2,1)S(1)}, u32[]{:S(2)}, u32[]{:S(2)}) collective-permute-start(bf16[96,128]{1,0:T(8,128)(2,1)S(1)} %first_samples.1.own0_ref), channel_id=1, source_target_pairs={{0,8},{1,9},{2,10},{3,11},{4,12},{5,13},{6,14},{7,15},{8,0},{9,1},... | collective-permute-start | bytes 73736 | tf_op jit(solution)/shard_map/ppermute | solution.py:412
  5.5 1.3 %collective-permute-start.1 = (bf16[96,128]{1,0:T(8,128)(2,1)S(1)}, bf16[96,128]{1,0:T(8,128)(2,1)S(1)}, u32[]{:S(2)}, u32[]{:S(2)}) collective-permute-start(bf16[96,128]{1,0:T(8,128)(2,1)S(1)} %first_samples.1.own0_ref), channel_id=1, source_target_pairs={{0,12},{1,13},{2,14},{3,15},{4,8},{5,9},{6,10},{7,11},{8,4},{9,5},... | collective-permute-start | bytes 73736 | tf_op jit(solution)/shard_map/ppermute | solution.py:412
  6.8 0.2 collective-permute-start
  7.1 0.0 copy-done
  7.1 0.6 %local_samples.1 = (bf16[192,4096]{1,0:T(8,128)(2,1)S(1)}, bf16[48,4096]{1,0:T(8,128)(2,1)S(1)}, bf16[480,128]{1,0:T(8,128)(2,1)S(1)}) custom-call(s32[1,21]{1,0:T(1,128)S(1)} %bitcast.3, f32[192,4096]{1,0:T(8,128)S(1)} %copy-done, bf16[96,128]{1,0:T(8,128)(2,1)S(1)} %first_samples.1.own0_ref), custom_call_target="tpu_custom_call" | custom-call | flops 1000 | bytes 1000 | tf_op jit(solution)/shard_map/local_samples/pallas_call | solution.py:441
  7.7 1.6 %collective-permute-start.6 = (bf16[480,128]{1,0:T(8,128)(2,1)S(1)}, bf16[480,128]{1,0:T(8,128)(2,1)S(1)}, u32[]{:S(2)}, u32[]{:S(2)}) collective-permute-start(bf16[480,128]{1,0:T(8,128)(2,1)S(1)} %get-tuple-element.42.refs_0_), channel_id=1, source_target_pairs={{0,2},{1,3},{2,0},{3,1},{4,6},{5,7},{6,4},{7,5},{8,10},{9,11},{10,... | collective-permute-start | bytes 368648 | tf_op jit(solution)/shard_map/ppermute | solution.py:412
  9.3 0.0 collective-permute-done.2
  9.3 1.8 %collective-permute-done.1 = bf16[96,128]{1,0:T(8,128)(2,1)S(1)} collective-permute-done((bf16[96,128]{1,0:T(8,128)(2,1)S(1)}, bf16[96,128]{1,0:T(8,128)(2,1)S(1)}, u32[]{:S(2)}, u32[]{:S(2)}) %collective-permute-start.1) | collective-permute-done | bytes 24608 | tf_op jit(solution)/shard_map/ppermute | solution.py:412
  11.1 0.0 collective-permute-done
  11.1 0.1 collective-permute-start.4
  11.2 1.6 %collective-permute-start.3 = (bf16[288,128]{1,0:T(8,128)(2,1)S(1)}, bf16[288,128]{1,0:T(8,128)(2,1)S(1)}, u32[]{:S(2)}, u32[]{:S(2)}) collective-permute-start(bf16[288,128]{1,0:T(8,128)(2,1)S(1)} %constant_dynamic-update-slice_fusion.refs_4_), channel_id=1, source_target_pairs={{0,2},{1,3},{2,0},{3,1},{4,6},{5,7},{6,4},{7,5},{8,10},{9,11},{10,... | collective-permute-start | bytes 221192 | tf_op jit(solution)/shard_map/ppermute | solution.py:412
  12.8 0.2 collective-permute-start.7
  13.0 0.0 copy-done.2
  13.0 0.0 copy-done.1
  13.0 0.8 %chosen_modes.1 = (f32[3,32,48]{2,1,0:T(8,128)S(1)}, f32[96,144]{1,0:T(8,128)S(1)}, f32[32,192]{1,0:T(8,128)S(1)}) custom-call(s32[1,21]{1,0:T(1,128)S(1)} %bitcast.4, f32[21,48,48]{2,1,0:T(8,128)S(1)} %copy-done.1, s32[21,32]{1,0:T(8,128)S(1)} %copy-done.2), custom_call_target="tpu_custom_call" | custom-call | flops 1000 | bytes 1000 | tf_op jit(solution)/shard_map/chosen_modes/pallas_call | solution.py:458
  13.8 0.0 collective-permute-done.6.refs_1_
  13.8 0.4 %collective-permute-start.8 = (bf16[480,128]{1,0:T(8,128)(2,1)S(1)}, bf16[480,128]{1,0:T(8,128)(2,1)S(1)}, u32[]{:S(2)}, u32[]{:S(2)}) collective-permute-start(bf16[480,128]{1,0:T(8,128)(2,1)S(1)} %collective-permute-done.6.refs_1_), channel_id=1, source_target_pairs={{0,1},{1,0},{2,3},{3,2},{4,5},{5,4},{6,7},{7,6},{8,9},{9,8},{10,11... | collective-permute-start | bytes 368648 | tf_op jit(solution)/shard_map/ppermute | solution.py:412
  14.2 0.0 collective-permute-done.4.refs_6_.far2_ref
  14.2 1.7 %collective-permute-done.3.refs_5_ = bf16[288,128]{1,0:T(8,128)(2,1)S(1)} collective-permute-done((bf16[288,128]{1,0:T(8,128)(2,1)S(1)}, bf16[288,128]{1,0:T(8,128)(2,1)S(1)}, u32[]{:S(2)}, u32[]{:S(2)}) %collective-permute-start.3) | collective-permute-done | bytes 73760 | tf_op jit(solution)/shard_map/ppermute | solution.py:412
  15.9 0.0 collective-permute-start.5
  15.9 0.0 collective-permute-done.7.refs_2_
  15.9 0.0 collective-permute-done.8.refs_3_.near3_ref
  15.9 1.1 %level_1_gram.1 = (f32[48,48]{1,0:T(8,128)S(1)}, bf16[128,4096]{1,0:T(8,128)(2,1)S(1)}) custom-call(bf16[48,4096]{1,0:T(8,128)(2,1)S(1)} %get-tuple-element.41.sel_ref, bf16[480,128]{1,0:T(8,128)(2,1)S(1)} %get-tuple-element.42.refs_0_, bf16[480,128]{1,0:T(8,128)(2,1)S(1)} %collective-permute-done.6.refs_1_, ...), custom_call_target="tpu_custom_call" | custom-call | flops 1000 | bytes 1000 | tf_op jit(solution)/shard_map/level_1_gram/pallas_call | solution.py:483
  17.0 0.1 collective-permute-done.5.far3_ref
  17.2 1.9 %cross_products.1 = (f32[96,256]{1,0:T(8,128)S(1)}, bf16[16,4096]{1,0:T(8,128)(2,1)S(1)}) custom-call(bf16[192,4096]{1,0:T(8,128)(2,1)S(1)} %get-tuple-element.34.round_ref, bf16[128,4096]{1,0:T(8,128)(2,1)S(1)} %get-tuple-element.51.early_ref, f32[48,48]{1,0:T(8,128)S(1)} %get-tuple-element.52.gram_ref, f32[96,144]{1,0:T(8,128)S(1)} %get-tuple-element.53.bd_ref, ...), custom_call_target="tpu_custom_call" | custom-call | flops 1000000000 | bytes 3000000 | tf_op jit(solution)/shard_map/cross_products/pallas_call | solution.py:496
  19.0 1.6 %collective-permute-start.9 = (f32[96,256]{1,0:T(8,128)S(1)}, f32[96,256]{1,0:T(8,128)S(1)}, u32[]{:S(2)}, u32[]{:S(2)}) collective-permute-start(f32[96,256]{1,0:T(8,128)S(1)} %get-tuple-element.56.w_ref), channel_id=1, source_target_pairs={{0,16},{16,0},{1,17},{17,1},{2,18},{18,2},{3,19},{19,3},{4,20},{20... | collective-permute-start | bytes 294920 | tf_op jit(solution)/shard_map/ppermute | solution.py:512
  20.6 3.6 %collective-permute-done.9.got_ref = f32[96,256]{1,0:T(8,128)S(1)} collective-permute-done((f32[96,256]{1,0:T(8,128)S(1)}, f32[96,256]{1,0:T(8,128)S(1)}, u32[]{:S(2)}, u32[]{:S(2)}) %collective-permute-start.9) | collective-permute-done | bytes 98336 | tf_op jit(solution)/shard_map/ppermute | solution.py:512
  24.2 5.8 %remove_slow.1 = f32[192,4096]{1,0:T(8,128)} custom-call(f32[96,256]{1,0:T(8,128)S(1)} %get-tuple-element.56.w_ref, f32[96,256]{1,0:T(8,128)S(1)} %collective-permute-done.9.got_ref, f32[3,32,48]{2,1,0:T(8,128)S(1)} %get-tuple-element.57.bt_ref, f32[192,4096]{1,0:T(8,128)S(1)} %copy-done, bf16[128,4096]{1,0:T(8,128)(2,1)S(1)} %get-tuple-element.51.early_ref, ...), custom_call_target="tpu_custom_call" | custom-call | flops 1000000000 | bytes 9000000 | tf_op jit(solution)/shard_map/remove_slow/pallas_call | solution.py:517
  (6 shorter events, 0.0 us)
Async XLA Ops:
  0.0 7.1 %copy-start = (f32[192,4096]{1,0:T(8,128)S(1)}, f32[192,4096]{1,0:T(8,128)}, u32[]{:S(2)}) copy-start(f32[192,4096]{1,0:T(8,128)} %x_ref.3) | copy-start | bytes 9437188
  0.0 1.1 %copy-start.3 = (s32[21]{0:T(128)S(1)}, s32[21]{0:T(128)}, u32[]{:S(2)}) copy-start(s32[21]{0:T(128)} %param.7) | copy-start | bytes 256
  0.0 13.0 %copy-start.2 = (s32[21,32]{1,0:T(8,128)S(1)}, s32[21,32]{1,0:T(8,128)}, u32[]{:S(2)}) copy-start(s32[21,32]{1,0:T(8,128)} %picks_ref.1) | copy-start | bytes 8068
  0.0 13.0 %copy-start.1 = (f32[21,48,48]{2,1,0:T(8,128)S(1)}, f32[21,48,48]{2,1,0:T(8,128)}, u32[]{:S(2)}) copy-start(f32[21,48,48]{2,1,0:T(8,128)} %basis_hbm.1) | copy-start | bytes 580612
  1.4 7.9 %collective-permute-start.2 = (bf16[96,128]{1,0:T(8,128)(2,1)S(1)}, bf16[96,128]{1,0:T(8,128)(2,1)S(1)}, u32[]{:S(2)}, u32[]{:S(2)}) collective-permute-start(bf16[96,128]{1,0:T(8,128)(2,1)S(1)} %first_samples.1.own0_ref), channel_id=1, source_target_pairs={{0,8},{1,9},{2,10},{3,11},{4,12},{5,13},{6,14},{7,15},{8,0},{9,1},... | collective-permute-start | bytes 73736 | tf_op jit(solution)/shard_map/ppermute | solution.py:412
  5.5 5.6 %collective-permute-start.1 = (bf16[96,128]{1,0:T(8,128)(2,1)S(1)}, bf16[96,128]{1,0:T(8,128)(2,1)S(1)}, u32[]{:S(2)}, u32[]{:S(2)}) collective-permute-start(bf16[96,128]{1,0:T(8,128)(2,1)S(1)} %first_samples.1.own0_ref), channel_id=1, source_target_pairs={{0,12},{1,13},{2,14},{3,15},{4,8},{5,9},{6,10},{7,11},{8,4},{9,5},... | collective-permute-start | bytes 73736 | tf_op jit(solution)/shard_map/ppermute | solution.py:412
  6.8 4.3 %collective-permute-start = (bf16[96,128]{1,0:T(8,128)(2,1)S(1)}, bf16[96,128]{1,0:T(8,128)(2,1)S(1)}, u32[]{:S(2)}, u32[]{:S(2)}) collective-permute-start(bf16[96,128]{1,0:T(8,128)(2,1)S(1)} %first_samples.1.own0_ref), channel_id=1, source_target_pairs={{0,4},{1,5},{2,6},{3,7},{4,0},{5,1},{6,2},{7,3},{8,12},{9,13},{10,... | collective-permute-start | bytes 73736 | tf_op jit(solution)/shard_map/ppermute | solution.py:412
  7.7 6.1 %collective-permute-start.6 = (bf16[480,128]{1,0:T(8,128)(2,1)S(1)}, bf16[480,128]{1,0:T(8,128)(2,1)S(1)}, u32[]{:S(2)}, u32[]{:S(2)}) collective-permute-start(bf16[480,128]{1,0:T(8,128)(2,1)S(1)} %get-tuple-element.42.refs_0_), channel_id=1, source_target_pairs={{0,2},{1,3},{2,0},{3,1},{4,6},{5,7},{6,4},{7,5},{8,10},{9,11},{10,... | collective-permute-start | bytes 368648 | tf_op jit(solution)/shard_map/ppermute | solution.py:412
  11.1 3.1 %collective-permute-start.4 = (bf16[288,128]{1,0:T(8,128)(2,1)S(1)}, bf16[288,128]{1,0:T(8,128)(2,1)S(1)}, u32[]{:S(2)}, u32[]{:S(2)}) collective-permute-start(bf16[288,128]{1,0:T(8,128)(2,1)S(1)} %constant_dynamic-update-slice_fusion.refs_4_), channel_id=1, source_target_pairs={{0,1},{1,0},{2,3},{3,2},{4,5},{5,4},{6,7},{7,6},{8,9},{9,8},{10,11... | collective-permute-start | bytes 221192 | tf_op jit(solution)/shard_map/ppermute | solution.py:412
  11.2 4.7 %collective-permute-start.3 = (bf16[288,128]{1,0:T(8,128)(2,1)S(1)}, bf16[288,128]{1,0:T(8,128)(2,1)S(1)}, u32[]{:S(2)}, u32[]{:S(2)}) collective-permute-start(bf16[288,128]{1,0:T(8,128)(2,1)S(1)} %constant_dynamic-update-slice_fusion.refs_4_), channel_id=1, source_target_pairs={{0,2},{1,3},{2,0},{3,1},{4,6},{5,7},{6,4},{7,5},{8,10},{9,11},{10,... | collective-permute-start | bytes 221192 | tf_op jit(solution)/shard_map/ppermute | solution.py:412
  12.8 3.1 %collective-permute-start.7 = (bf16[480,128]{1,0:T(8,128)(2,1)S(1)}, bf16[480,128]{1,0:T(8,128)(2,1)S(1)}, u32[]{:S(2)}, u32[]{:S(2)}) collective-permute-start(bf16[480,128]{1,0:T(8,128)(2,1)S(1)} %get-tuple-element.42.refs_0_), channel_id=1, source_target_pairs={{0,1},{1,0},{2,3},{3,2},{4,5},{5,4},{6,7},{7,6},{8,9},{9,8},{10,11... | collective-permute-start | bytes 368648 | tf_op jit(solution)/shard_map/ppermute | solution.py:412
  13.8 2.1 %collective-permute-start.8 = (bf16[480,128]{1,0:T(8,128)(2,1)S(1)}, bf16[480,128]{1,0:T(8,128)(2,1)S(1)}, u32[]{:S(2)}, u32[]{:S(2)}) collective-permute-start(bf16[480,128]{1,0:T(8,128)(2,1)S(1)} %collective-permute-done.6.refs_1_), channel_id=1, source_target_pairs={{0,1},{1,0},{2,3},{3,2},{4,5},{5,4},{6,7},{7,6},{8,9},{9,8},{10,11... | collective-permute-start | bytes 368648 | tf_op jit(solution)/shard_map/ppermute | solution.py:412
  15.9 1.3 %collective-permute-start.5 = (bf16[288,128]{1,0:T(8,128)(2,1)S(1)}, bf16[288,128]{1,0:T(8,128)(2,1)S(1)}, u32[]{:S(2)}, u32[]{:S(2)}) collective-permute-start(bf16[288,128]{1,0:T(8,128)(2,1)S(1)} %collective-permute-done.3.refs_5_), channel_id=1, source_target_pairs={{0,1},{1,0},{2,3},{3,2},{4,5},{5,4},{6,7},{7,6},{8,9},{9,8},{10,11... | collective-permute-start | bytes 221192 | tf_op jit(solution)/shard_map/ppermute | solution.py:412
  19.0 5.1 %collective-permute-start.9 = (f32[96,256]{1,0:T(8,128)S(1)}, f32[96,256]{1,0:T(8,128)S(1)}, u32[]{:S(2)}, u32[]{:S(2)}) collective-permute-start(f32[96,256]{1,0:T(8,128)S(1)} %get-tuple-element.56.w_ref), channel_id=1, source_target_pairs={{0,16},{16,0},{1,17},{17,1},{2,18},{18,2},{3,19},{19,3},{4,20},{20... | collective-permute-start | bytes 294920 | tf_op jit(solution)/shard_map/ppermute | solution.py:512
